TPU v7x, 32 devices: a whole 2x2x4 slice. The times are simulated.
32 devices in a mesh: fsdp: 4 (over y, x), seq: 8 (over z, core).
Axes of the slice: x: 2, y: 2, z: 4, core: 2. Of those that a mesh axis runs over, the one named last changes fastest.
Arguments:
- tokens: bfloat16 [8192, 2048], P(('fsdp', 'seq')), may hold values from -6 to 6
- seq_lengths: int32 [4, 4], P('fsdp'), may hold values from 1 to 1024, 2048 in all within a row
- in_weight: bfloat16 [2048, 6144], P(None, 'fsdp'), may hold values from -0.125 to 0.125
- short_filter: float32 [7, 6144], replicated, may hold values from -2.5 to 2.5
- long_filter: bfloat16 [128, 128], replicated, may hold values from -0.5 to 0.5
- out_weight: bfloat16 [2048, 2048], replicated, may hold values from -0.125 to 0.125
Outputs:
- mixed: bfloat16 [8192, 2048], P(('fsdp', 'seq'))
Inputs may be any that keep to these rules, and one draw needn't show every extreme that they name: `seq_lengths`: in each pack the 4 lengths sum to 2048 and the longest is exactly 1024.
All inputs are finite; a program needn't handle non-finite values.
Results may differ from a plain program's by a relative error of at most 0.0073.
Values may be sent and summed in bfloat16 or wider, within the bound.
A program may use at most 128 MiB of HBM per device.

v0:
```python
import jax
import jax.numpy as jnp
from jax import lax
from jax.sharding import PartitionSpec as P


def from_behind(block, axis, distance):
    devices = range(lax.axis_size(axis))
    route = [(i - distance, i) for i in devices if i - distance in devices]
    return lax.ppermute(block, axis, route)


def positions(row_ids, seq_starts):
    seq_begin = jnp.max(
        jnp.where(seq_starts[None, :] <= row_ids[:, None], seq_starts[None, :], 0), axis=1
    )
    return row_ids - seq_begin


def featurize(extended, position, taps):
    width = taps.shape[0]
    rows = position.shape[0]
    total = jnp.zeros((rows, extended.shape[1]), jnp.float32)
    for tap_index in range(width):
        part = extended[width - 1 - tap_index : width - 1 - tap_index + rows].astype(jnp.float32)
        total = total + taps[tap_index] * jnp.where((position >= tap_index)[:, None], part, 0.0)
    return total


def tap_table(tap_ids, long_filter):
    filter_len = long_filter.shape[0]
    one_hot = (
        tap_ids[:, :, None] == jnp.arange(filter_len, dtype=jnp.int32)[None, None, :]
    ).astype(jnp.bfloat16)
    return jnp.einsum(
        "ijt,tg->ijg", one_hot, long_filter, preferred_element_type=jnp.float32
    ).astype(jnp.bfloat16)


def local(tokens, seq_lengths, in_weight, short_filter, long_filter, out_weight):
    row_count, channels = tokens.shape
    width = short_filter.shape[0]
    filter_len, group_count = long_filter.shape
    projected = jnp.dot(
        tokens,
        lax.all_gather(in_weight, "fsdp", axis=1, tiled=True),
        preferred_element_type=jnp.float32,
    ).astype(jnp.bfloat16)
    lengths_row = seq_lengths[0]
    seq_starts = jnp.cumsum(lengths_row) - lengths_row
    first_global = lax.axis_index("seq") * row_count
    row_ids = first_global + jnp.arange(row_count, dtype=jnp.int32)
    position = positions(row_ids, seq_starts)
    prev_tail = from_behind(projected[row_count - (width - 1) :], "seq", 1)
    extended = jnp.concatenate([prev_tail, projected], axis=0)
    featured = featurize(extended, position, short_filter)
    queries = featured[:, :channels]
    mixed_in = (featured[:, channels : 2 * channels] * featured[:, 2 * channels :]).astype(
        jnp.bfloat16
    )
    conv_tail = from_behind(mixed_in[row_count - (filter_len - 1) :], "seq", 1)
    window_all = jnp.concatenate([conv_tail, mixed_in], axis=0)
    out_rows = jnp.arange(filter_len, dtype=jnp.int32)[:, None]
    cur_tap = out_rows - jnp.arange(filter_len, dtype=jnp.int32)[None, :]
    prev_tap = out_rows + (filter_len - 1) - jnp.arange(filter_len - 1, dtype=jnp.int32)[None, :]
    cur_table = tap_table(cur_tap, long_filter)
    prev_table = tap_table(prev_tap, long_filter)
    per_group = channels // group_count
    pieces = []
    for block_id in range(row_count // filter_len):
        first_row = block_id * filter_len
        block_pos = position[first_row : first_row + filter_len]
        cur_kernel = jnp.where((cur_tap <= block_pos[:, None])[:, :, None], cur_table, 0.0)
        prev_kernel = jnp.where((prev_tap <= block_pos[:, None])[:, :, None], prev_table, 0.0)
        prev_src = window_all[first_row : first_row + filter_len - 1].reshape(
            filter_len - 1, group_count, per_group
        )
        cur_src = window_all[first_row + filter_len - 1 : first_row + 2 * filter_len - 1].reshape(
            filter_len, group_count, per_group
        )
        block_out = jnp.einsum(
            "ijg,jgc->igc", cur_kernel, cur_src, preferred_element_type=jnp.float32
        )
        block_out = block_out + jnp.einsum(
            "ijg,jgc->igc", prev_kernel, prev_src, preferred_element_type=jnp.float32
        )
        pieces.append(block_out.reshape(filter_len, channels))
    filtered = jnp.concatenate(pieces, axis=0)
    gated_out = (queries * filtered).astype(jnp.bfloat16)
    result = tokens.astype(jnp.float32) + jnp.dot(
        gated_out, out_weight, preferred_element_type=jnp.float32
    )
    return result.astype(jnp.bfloat16)


def solution(mesh):
    in_specs = (P(("fsdp", "seq"), None), P("fsdp", None), P(None, "fsdp"), P(), P(), P())
    out_specs = P(("fsdp", "seq"), None)
    return jax.shard_map(local, mesh=mesh, in_specs=in_specs, out_specs=out_specs, check_vma=False)
```

profile of v0, /device:TPU:0, one launch (start us, length us, event | category | flops | bytes accessed | tf_op | source)
XLA Modules:
  0.0 332.5 jit_solution(5312147125077584268)
XLA Ops:
  6.5 0.7 all-gather.2.cloned.1.call-update
  7.8 8.9 %broadcast_select_fusion.3 = (bf16[128,127,128]{2,0,1:T(8,128)(2,1)}, bf16[128,127,128]{2,0,1:T(8,128)(2,1)}) fusion(pred[128,127]{0,1:T(8,128)(4,1)S(1)} %get-tuple-element.30, pred[128,127]{0,1:T(8,128)(4,1)S(1)} %get-tuple-element.31, bf16[128,128]{1,0:T(8,128)(2,1)S(1)} %copy-done, s32[128,127]{0,1:T(8,128)S(1)} %iota_subtract_fusion), kind=kOutput, calls=%fused_computation.16 | convolution fusion | flops 540999680 | bytes 8453376 | tf_op jit(solution)/shard_map/ijt,tg->ijg/dot_general | solution.py:35
  16.6 10.4 %broadcast_select_fusion.1 = (bf16[128,128,128]{2,1,0:T(8,128)(2,1)}, bf16[128,128,128]{2,1,0:T(8,128)(2,1)}) fusion(pred[128,128]{1,0:T(8,128)(4,1)S(1)} %get-tuple-element.33, pred[128,128]{1,0:T(8,128)(4,1)S(1)} %get-tuple-element.32, bf16[128,128]{1,0:T(8,128)(2,1)S(1)} %copy-done, s32[128,128]{1,0:T(8,128)S(1)} %iota_subtract_fusion.1), kind=kOutput, calls=%fused_computation.13 | convolution fusion | flops 545259520 | bytes 8519680 | tf_op jit(solution)/shard_map/ijt,tg->ijg/dot_general | solution.py:35
  27.1 212.5 %all-gather.2.cloned.1.call-done = bf16[2048,6144]{1,0:T(8,128)(2,1)} async-done(((bf16[2048,1536]{1,0:T(8,128)(2,1)}), bf16[2048,6144]{1,0:T(8,128)(2,1)}) %all-gather.2.cloned.1.call-update) | async-done | bytes 25165840 | tf_op jit(solution)/shard_map/all_gather | solution.py:46
  239.7 11.9 %convolution_convert_fusion = bf16[256,6144]{1,0:T(8,128)(2,1)S(1)} fusion(bf16[256,2048]{1,0:T(8,128)(2,1)} %param.6, bf16[2048,6144]{1,0:T(8,128)(2,1)} %all-gather.2.cloned.1.call-done), kind=kOutput, calls=%fused_computation.9 | convolution fusion | flops 6444023808 | bytes 29360128 | tf_op jit(solution)/shard_map/dot_general | solution.py:44
  251.6 1.7 collective-permute-start
  253.4 6.8 %copy.32 = bf16[128,128,128]{1,0,2:T(8,128)(2,1)} copy(bf16[128,128,128]{2,1,0:T(8,128)(2,1)} %get-tuple-element.8) | data formatting | bytes 8388608 | tf_op jit(solution)/shard_map/jit(_where)/select_n | solution.py:73
  260.1 7.2 %copy.34 = bf16[128,127,128]{1,0,2:T(8,128)(2,1)} copy(bf16[128,127,128]{2,0,1:T(8,128)(2,1)} %get-tuple-element.10) | data formatting | bytes 8323072 | tf_op jit(solution)/shard_map/jit(_where)/select_n | solution.py:74
  267.3 6.7 %copy.28 = bf16[128,128,128]{1,0,2:T(8,128)(2,1)} copy(bf16[128,128,128]{2,1,0:T(8,128)(2,1)} %get-tuple-element.7) | data formatting | bytes 8388608 | tf_op jit(solution)/shard_map/jit(_where)/select_n | solution.py:73
  274.0 7.1 %copy.30 = bf16[128,127,128]{1,0,2:T(8,128)(2,1)} copy(bf16[128,127,128]{2,0,1:T(8,128)(2,1)} %get-tuple-element.9) | data formatting | bytes 8323072 | tf_op jit(solution)/shard_map/jit(_where)/select_n | solution.py:74
  281.1 9.8 %multiply_add_fusion = f32[256,6144]{1,0:T(8,128)S(1)} fusion(bf16[256,6144]{1,0:T(8,128)(2,1)S(1)} %convolution_convert_fusion, bf16[6,6144]{1,0:T(8,128)(2,1)S(1)} %collective-permute-done, f32[6144]{0:T(1024)S(1)} %bitcast.52, f32[6144]{0:T(1024)S(1)} %bitcast.53, f32[6144]{0:T(1024)S(1)} %bitcast.48, f32[6144]{0:T(1024)S(1)} %bitcast.49, ...), kind=kLoop, calls=%fused_computation.10 | loop fusion | flops 70778880 | bytes 9684736 | tf_op jit(solution)/shard_map/add | solution.py:26
  291.0 2.6 copy-done.2
  294.0 1.1 fusion.24
  295.3 0.3 copy.33
  295.6 4.1 %collective-permute-start.1 = (bf16[127,2048]{1,0:T(8,128)(2,1)}, bf16[127,2048]{1,0:T(8,128)(2,1)S(1)}, u32[]{:S(2)}, u32[]{:S(2)}) collective-permute-start(bf16[127,2048]{1,0:T(8,128)(2,1)} %get-tuple-element.11), channel_id=1, source_target_pairs={{0,1},{1,2},{2,3},{3,4},{4,5},{5,6},{6,7},{8,9},{9,10},{10,11},{11... | collective-permute-start | bytes 1560584 | tf_op jit(solution)/shard_map/ppermute | solution.py:10
  299.8 4.5 %fusion.29 = f32[128,16,128]{2,1,0:T(8,128)S(1)} fusion(bf16[128,128,16]{0,2,1:T(8,128)(2,1)S(1)} %bitcast.44, bf16[128,128,128]{1,0,2:T(8,128)(2,1)} %copy.32), kind=kOutput, calls=%fused_computation.62 | convolution fusion | flops 67108864 | bytes 5767168 | tf_op jit(solution)/shard_map/ijg,jgc->igc/dot_general | solution.py:81
  304.2 2.3 convolution_add_fusion.1
  306.5 1.4 copy.36
  307.9 0.3 copy.27
  308.2 4.5 %fusion.28 = f32[128,16,128]{2,1,0:T(8,128)S(1)} fusion(bf16[128,128,16]{0,2,1:T(8,128)(2,1)S(1)} %bitcast.46, bf16[128,128,128]{1,0,2:T(8,128)(2,1)} %copy.28), kind=kOutput, calls=%fused_computation.61 | convolution fusion | flops 67108864 | bytes 5767168 | tf_op jit(solution)/shard_map/ijg,jgc->igc/dot_general | solution.py:81
  312.6 0.3 copy.29
  312.9 4.4 %convolution_add_fusion.2 = f32[128,16,128]{2,1,0:T(8,128)S(1)} fusion(f32[128,16,128]{2,1,0:T(8,128)S(1)} %fusion.28, bf16[127,128,16]{0,2,1:T(8,128)(2,1)S(1)} %bitcast.45, bf16[128,127,128]{1,0,2:T(8,128)(2,1)} %copy.30), kind=kOutput, calls=%fused_computation.35 | convolution fusion | flops 66846720 | bytes 6778880 | tf_op jit(solution)/shard_map/ijg,jgc->igc/dot_general | solution.py:84
  317.4 0.4 copy.35
  317.7 7.9 %fusion.11 = bf16[256,2048]{1,0:T(8,128)(2,1)} fusion(bf16[2048,2048]{1,0:T(8,128)(2,1)} %param.11, bf16[256,2048]{1,0:T(8,128)(2,1)} %param.6, f32[256,6144]{1,0:T(8,128)} %copy-done.2, f32[128,2048]{1,0:T(8,128)} %copy.36, f32[128,2048]{1,0:T(8,128)S(1)} %copy.35), kind=kOutput, calls=%fused_computation.29 | convolution fusion | flops 2150629376 | bytes 14680064 | tf_op jit(solution)/shard_map/dot_general | solution.py:90
  (31 shorter events, 1.2 us)
Async XLA Ops:
  6.5 1.2 copy-start
  6.5 0.7 copy-start.5
  6.5 233.1 %all-gather.2.cloned.1.call-start = ((), (), s32[]{:S(2)}) async-start(), calls=%async_computation | async-start | bytes 31457280 | tf_op jit(solution)/shard_map/all_gather | solution.py:46
  16.6 10.4 %copy-start.4 = (f32[7,6144]{1,0:T(8,128)S(1)}, f32[7,6144]{1,0:T(8,128)}, u32[]{:S(2)}) copy-start(f32[7,6144]{1,0:T(8,128)} %param.9) | copy-start | bytes 516100
  251.6 29.6 %collective-permute-start = (bf16[6,6144]{1,0:T(8,128)(2,1)S(1)}, bf16[6,6144]{1,0:T(8,128)(2,1)S(1)}, u32[]{:S(2)}, u32[]{:S(2)}) collective-permute-start(bf16[6,6144]{1,0:T(8,128)(2,1)S(1)} %slice.92), channel_id=1, source_target_pairs={{0,1},{1,2},{2,3},{3,4},{4,5},{5,6},{6,7},{8,9},{9,10},{10,11},{11... | collective-permute-start | bytes 221192 | tf_op jit(solution)/shard_map/ppermute | solution.py:10
  291.0 2.7 copy-start.2
  295.6 8.6 %copy-start.3 = (bf16[128,127,128]{1,0,2:T(8,128)(2,1)S(1)}, bf16[128,127,128]{1,0,2:T(8,128)(2,1)}, u32[]{:S(2)}) copy-start(bf16[128,127,128]{1,0,2:T(8,128)(2,1)} %copy.34) | copy-start | bytes 12484612
  295.6 17.0 %collective-permute-start.1 = (bf16[127,2048]{1,0:T(8,128)(2,1)}, bf16[127,2048]{1,0:T(8,128)(2,1)S(1)}, u32[]{:S(2)}, u32[]{:S(2)}) collective-permute-start(bf16[127,2048]{1,0:T(8,128)(2,1)} %get-tuple-element.11), channel_id=1, source_target_pairs={{0,1},{1,2},{2,3},{3,4},{4,5},{5,6},{6,7},{8,9},{9,10},{10,11},{11... | collective-permute-start | bytes 1560584 | tf_op jit(solution)/shard_map/ppermute | solution.py:10
  317.7 7.9 %copy-start.1 = (bf16[128,128]{1,0:T(8,128)(2,1)S(1)}, bf16[128,128]{1,0:T(8,128)(2,1)}, u32[]{:S(2)}) copy-start(bf16[128,128]{1,0:T(8,128)(2,1)} %param.10) | copy-start | bytes 98308
Sparse Core Ops, SparseCore 0:
  9.2 230.3 all-gather.1
where the time goes:
time: 333 us; the launch traced here: 332 us
  waiting for transfers between devices  213 us (64%)
  matrix products  54.6 us (16%)
  local copies, waits for them, and re-layouts  34.6 us (10%)
  between operations  13.6 us (4%)
  other arithmetic  10.5 us (3%)
  starting transfers between devices  5.89 us (2%)
    all_gather x1, waiting for transfers between devices, local(): lax.all_gather(in_weight, 'fsdp', axis=1, tiled=True)  213 us
    dot_general x2, matrix products, tap_table(): jnp.einsum('ijt,tg->ijg', one_hot, long_filter, preferred_element_type=jn...  19.2 us
    select_n x2, local copies, waits for them, and re-layouts, local(): jnp.where((prev_tap <= block_pos[:, None])[:, :, None], prev_table, 0.0)  14.3 us
    select_n x2, local copies, waits for them, and re-layouts, local(): jnp.where((cur_tap <= block_pos[:, None])[:, :, None], cur_table, 0.0)  13.5 us
    dot_general x1, matrix products, local(): jnp.dot(tokens, lax.all_gather(in_weight, 'fsdp', axis=1, tiled=True), pr...  11.9 us
    add x1, other arithmetic, featurize(): total + taps[tap_index] * jnp.where((position >= tap_index)[:, None], par...  9.84 us
    dot_general x2, matrix products, local(): jnp.einsum('ijg,jgc->igc', cur_kernel, cur_src, preferred_element_type=jn...  8.91 us
    dot_general x1, matrix products, local(): jnp.dot(gated_out, out_weight, preferred_element_type=jnp.float32)  7.87 us
  transfers between devices with their start and end apart: 3, of which 1 were waited for; matrix products, arithmetic and copies ran while one was open for 18% of the time, Pallas kernels for 0%

commit v1 on v0

--- a/solution.py
+++ b/solution.py
@@ -1,6 +1,10 @@
+import functools
+
 import jax
 import jax.numpy as jnp
 from jax import lax
+from jax.experimental import pallas as pl
+from jax.experimental.pallas import tpu as pltpu
 from jax.sharding import PartitionSpec as P
 
 
@@ -93,7 +97,210 @@
     return result.astype(jnp.bfloat16)
 
 
+def role_kernel(tok_ref, own_ref, xm_ref, xo_ref, ym_ref, yo_ref, out_ref):
+    f = lax.axis_index("fsdp")
+    core = lax.rem(lax.axis_index("seq"), 2)
+    half = xm_ref.shape[1]
+    own_role = jnp.where(f == 0, 0, jnp.where(f == 3, 2, 1))
+    x_role = jnp.where(f == 1, 0, jnp.where(f == 2, 2, 1))
+    y_role = jnp.where(f < 2, 2, 0)
+    tok = tok_ref[...]
+
+    def put(role, column, weight):
+        columns = pl.ds(pl.multiple_of(column, half), half)
+        out_ref[role, :, columns] = jnp.dot(
+            tok, weight, preferred_element_type=jnp.float32
+        ).astype(jnp.bfloat16)
+
+    put(own_role, 0, own_ref[:, :half])
+    put(own_role, half, own_ref[:, half:])
+    mine, other = core * half, (1 - core) * half
+    put(x_role, mine, xm_ref[...])
+    put(x_role, other, xo_ref[...])
+    put(y_role, mine, ym_ref[...])
+    put(y_role, other, yo_ref[...])
+
+
+def project(tok, blocks):
+    rows, block = tok.shape[0], blocks[0].shape[1]
+    return pl.pallas_call(
+        role_kernel,
+        out_shape=jax.ShapeDtypeStruct((3, rows, block), jnp.bfloat16),
+        in_specs=[pl.BlockSpec(memory_space=pltpu.VMEM)] * 6,
+        out_specs=pl.BlockSpec(memory_space=pltpu.VMEM),
+        compiler_params=pltpu.CompilerParams(vmem_limit_bytes=40 << 20),
+        cost_estimate=pl.CostEstimate(
+            flops=2 * rows * tok.shape[1] * 3 * block,
+            bytes_accessed=2 * (tok.size + 3 * tok.shape[1] * block + 3 * rows * block),
+            transcendentals=0,
+        ),
+    )(tok, *blocks)
+
+
+def table_kernel(taps_ref, table_ref):
+    groups, window = taps_ref.shape
+    filter_len = window // 2
+    for g in range(groups):
+        row = jnp.broadcast_to(taps_ref[g : g + 1, :], (filter_len, window))
+        shifted = pltpu.roll(row, 0, 1, stride=1, stride_axis=0)
+        table_ref[g * filter_len : (g + 1) * filter_len, :] = shifted.astype(jnp.bfloat16)
+
+
+def toeplitz(taps):
+    groups, window = taps.shape
+    return pl.pallas_call(
+        table_kernel,
+        out_shape=jax.ShapeDtypeStruct((groups * window // 2, window), jnp.bfloat16),
+        in_specs=[pl.BlockSpec(memory_space=pltpu.VMEM)],
+        out_specs=pl.BlockSpec(memory_space=pltpu.VMEM),
+        compiler_params=pltpu.CompilerParams(vmem_limit_bytes=40 << 20),
+    )(taps)
+
+
+def mix_kernel(width, per_group, pos_ref, halo_ref, proj_ref, taps_ref, table_ref, out_ref,
+               ext_ref, mixed_ref, query_ref):
+    halo, rows, channels = halo_ref.shape[1], proj_ref.shape[1], proj_ref.shape[2]
+    window = table_ref.shape[1]
+    fl = window // 2
+    for role in range(3):
+        ext_ref[role, :halo, :] = halo_ref[role].astype(jnp.float32)
+        ext_ref[role, halo:, :] = proj_ref[role].astype(jnp.float32)
+
+    def feature(role, first, lanes, pos):
+        total = None
+        for t in range(width):
+            start = halo - fl + first - t
+            part = ext_ref[role, start : start + fl, lanes]
+            if t > 0:
+                part = jnp.where(pos >= t, part, 0.0)
+            term = taps_ref[role, t : t + 1, lanes] * part
+            total = term if total is None else total + term
+        return total
+
+    for first in range(0, rows + fl, fl):
+        pos = pos_ref[first : first + fl, :]
+        for lane in range(0, channels, 128):
+            lanes = slice(lane, lane + 128)
+            both = feature(1, first, lanes, pos) * feature(2, first, lanes, pos)
+            mixed_ref[first : first + fl, lanes] = both.astype(jnp.bfloat16)
+            if first >= fl:
+                query_ref[first - fl : first, lanes] = feature(0, first, lanes, pos)
+
+    side = 256
+    many = side // per_group
+    out_row = lax.broadcasted_iota(jnp.int32, (fl, window), 0)
+    source = lax.broadcasted_iota(jnp.int32, (fl, window), 1)
+    lane_group = lax.broadcasted_iota(jnp.int32, (fl, side), 1) // per_group
+    step = 8
+    for b in range(rows // fl):
+        pos = pos_ref[fl + b * fl : 2 * fl + b * fl, :]
+        keep = jnp.where(source >= fl + out_row - pos, 1.0, 0.0).astype(jnp.bfloat16)
+        for n in range(channels // side):
+            lanes = slice(n * side, (n + 1) * side)
+            src = mixed_ref[b * fl : b * fl + window, lanes]
+            total = jnp.zeros((fl, side), jnp.float32)
+            for g0 in range(0, many, step):
+                base = (n * many + g0) * fl
+                tab = table_ref[base : base + step * fl, :].reshape(step, fl, window)
+                tab = (tab * keep[None]).reshape(step * fl, window)
+                res = jnp.dot(tab, src, preferred_element_type=jnp.float32)
+                for g in range(step):
+                    total = jnp.where(lane_group == g0 + g, res[g * fl : (g + 1) * fl], total)
+            out_rows = slice(b * fl, (b + 1) * fl)
+            out_ref[out_rows, lanes] = (query_ref[out_rows, lanes] * total).astype(jnp.bfloat16)
+
+
+def mix(pos, halo, proj, taps, table, width, per_group):
+    _, rows, channels = proj.shape
+    fl = table.shape[1] // 2
+    return pl.pallas_call(
+        functools.partial(mix_kernel, width, per_group),
+        out_shape=jax.ShapeDtypeStruct((rows, channels), jnp.bfloat16),
+        in_specs=[pl.BlockSpec(memory_space=pltpu.VMEM)] * 5,
+        out_specs=pl.BlockSpec(memory_space=pltpu.VMEM),
+        scratch_shapes=[
+            pltpu.VMEM((3, halo.shape[1] + rows, channels), jnp.float32),
+            pltpu.VMEM((fl + rows, channels), jnp.bfloat16),
+            pltpu.VMEM((rows, channels), jnp.float32),
+        ],
+        compiler_params=pltpu.CompilerParams(vmem_limit_bytes=40 << 20),
+        cost_estimate=pl.CostEstimate(
+            flops=4 * rows * table.size // 2,
+            bytes_accessed=2 * (table.size + halo.size + 4 * proj.size),
+            transcendentals=0,
+        ),
+    )(pos, halo, proj, taps, table)
+
+
+def swap(block, bit):
+    return lax.ppermute(block, "fsdp", [(i, i ^ bit) for i in range(4)])
+
+
+def swap_cores(block):
+    return lax.ppermute(block, "seq", [(i, i ^ 1) for i in range(lax.axis_size("seq"))])
+
+
+def local_four(tokens, seq_lengths, in_weight, short_filter, long_filter, out_weight):
+    rows, channels = tokens.shape
+    width = short_filter.shape[0]
+    filter_len, group_count = long_filter.shape
+    per_group = channels // group_count
+    f = lax.axis_index("fsdp")
+    seq = lax.axis_index("seq")
+    core = seq % 2
+    block = channels // 4
+    half = block // 2
+    groups = group_count // 4
+
+    tok_x = swap(tokens, 1)
+    tok_y = swap(tokens, 2)
+    odd = f % 2
+    own = lax.dynamic_slice(in_weight, (0, odd * 2 * block), (channels, block))
+    x_send = lax.dynamic_slice(in_weight, (0, block + core * half), (channels, half))
+    y_send = lax.dynamic_slice(in_weight, (0, (1 - odd) * 2 * block + core * half), (channels, half))
+    x_mine = swap(x_send, 1)
+    y_mine = swap(y_send, 2)
+    x_other = swap_cores(x_mine)
+    y_other = swap_cores(y_mine)
+    tok_d = jnp.concatenate(
+        [swap(tok_x[: rows // 2], 2), swap(tok_y[rows // 2 :], 1)], axis=0
+    )
+    blocks = (own, x_mine, x_other, y_mine, y_other)
+
+    lengths = lax.all_gather(seq_lengths, "fsdp", axis=0, tiled=True)
+    seq_starts = jnp.cumsum(lengths, axis=1) - lengths
+    row_ids = seq * rows - filter_len + jnp.arange(rows + filter_len, dtype=jnp.int32)
+    taps = lax.dynamic_slice(
+        short_filter.reshape(width, 3, 4, block), (0, 0, f, 0), (width, 3, 1, block)
+    )[:, :, 0].transpose(1, 0, 2)
+    own_filter = lax.dynamic_slice(long_filter, (0, f * groups), (filter_len, groups))
+    reverse = jnp.flip(own_filter.astype(jnp.float32), 0).T
+    table = toeplitz(jnp.pad(reverse, ((0, 0), (1, filter_len - 1))))
+
+    halo_rows = filter_len + 16
+    gated = []
+    for bit, tok in ((0, tokens), (1, tok_x), (2, tok_y), (3, tok_d)):
+        proj = project(tok, blocks)
+        halo = from_behind(proj[:, rows - halo_rows :], "seq", 1)
+        starts = lax.dynamic_slice(seq_starts, (f ^ bit, 0), (1, seq_starts.shape[1]))[0]
+        pos = positions(row_ids, starts)[:, None]
+        out = mix(pos, halo, proj, taps, table, width, per_group)
+        gated.append(out if bit == 0 else swap(out, bit))
+
+    def rows_of(bit):
+        return lax.dynamic_slice(out_weight, ((f ^ bit) * block, 0), (block, channels))
+
+    first = jnp.concatenate(gated[:3], axis=1)
+    first_weight = jnp.concatenate([rows_of(0), rows_of(1), rows_of(2)], axis=0)
+    result = tokens.astype(jnp.float32) + jnp.dot(
+        first, first_weight, preferred_element_type=jnp.float32
+    )
+    result = result + jnp.dot(gated[3], rows_of(3), preferred_element_type=jnp.float32)
+    return result.astype(jnp.bfloat16)
+
+
 def solution(mesh):
     in_specs = (P(("fsdp", "seq"), None), P("fsdp", None), P(None, "fsdp"), P(), P(), P())
     out_specs = P(("fsdp", "seq"), None)
-    return jax.shard_map(local, mesh=mesh, in_specs=in_specs, out_specs=out_specs, check_vma=False)
+    body = local_four if mesh.shape["fsdp"] == 4 and mesh.shape["seq"] % 2 == 0 else local
+    return jax.shard_map(body, mesh=mesh, in_specs=in_specs, out_specs=out_specs, check_vma=False)

time: 333 us -> 141 us (0.42)
  waiting for transfers between devices: 213 us -> 3.33 us
  matrix products: 54.6 us -> 6.39 us
  blocking collectives: 0 us -> 47.2 us
  Pallas kernels: 0 us -> 33.3 us
  starting transfers between devices: 5.89 us -> 23.9 us
  between operations: 13.6 us -> 0.37 us
  local copies, waits for them, and re-layouts: 34.6 us -> 22.2 us
  other arithmetic: 10.5 us -> 3.86 us
    all_gather x1 -> x0, waiting for transfers between devices: 213 us -> none  [local(): lax.all_gather(in_weight, 'fsdp', axis=1, tiled=True)]
    dot_general x8 -> x2, matrix products: 54.6 us -> 6.39 us  [the longest x1 3.94 us: local_four(): jnp.dot(first, first_weight, preferred_element_type=jnp.float32)]
    all_gather x0 -> x1, blocking collectives: none -> 47.2 us  [local_four(): lengths = lax.all_gather(seq_lengths, 'fsdp', axis=0, tiled=True)]
    pallas_call x0 -> x9, Pallas kernels: none -> 33.3 us  [the longest x4 17.8 us: mix(): pl.pallas_call(functools.partial(mix_kernel, width, per_group), out_shape...]
    select_n x4 -> x0, local copies, waits for them, and re-layouts: 27.8 us -> none  [the longest x2 14.3 us: local(): jnp.where((prev_tap <= block_pos[:, None])[:, :, None], prev_table, 0.0)]
    ppermute x0 -> x11, starting transfers between devices: none -> 12.4 us  [the longest x9 11.9 us: swap(): return lax.ppermute(block, 'fsdp', [(i, i ^ bit) for i in range(4)])]
    dynamic_slice x0 -> x5, local copies, waits for them, and re-layouts: none -> 12 us  [the longest x1 5.7 us: rows_of(): lax.dynamic_slice(out_weight, ((f ^ bit) * block, 0), (block, channels))]
    add x3 -> x1, other arithmetic: 9.84 us -> 0.01 us  [local_four(): seq * rows - filter_len + jnp.arange(rows + filter_len, dtype=jnp.int32)]
  transfers between devices with their start and end apart: 3 -> 15, of which waited for: 1 -> 2; matrix products, arithmetic and copies ran while one was open for 18% -> 15% of each run, Pallas kernels for 0% -> 21%
where the time goes in v1:
time: 141 us
  blocking collectives  47.2 us (33%)
  Pallas kernels  33.3 us (24%)
  starting transfers between devices  23.9 us (17%)
  local copies, waits for them, and re-layouts  22.2 us (16%)
  matrix products  6.39 us (5%)
  other arithmetic  3.86 us (3%)
  waiting for transfers between devices  3.33 us (2%)
    all_gather x1, blocking collectives, local_four(): lengths = lax.all_gather(seq_lengths, 'fsdp', axis=0, tiled=True)  47.2 us
    pallas_call x4, Pallas kernels, mix(): pl.pallas_call(functools.partial(mix_kernel, width, per_group), out_shape...  17.8 us
    pallas_call x4, Pallas kernels, project(): pl.pallas_call(role_kernel, out_shape=jax.ShapeDtypeStruct((3, rows, bloc...  14.9 us
    ppermute x9, starting transfers between devices, swap(): return lax.ppermute(block, 'fsdp', [(i, i ^ bit) for i in range(4)])  11.9 us
    ppermute x4, starting transfers between devices, from_behind(): return lax.ppermute(block, axis, route)  11.5 us
    dynamic_slice x1, local copies, waits for them, and re-layouts, rows_of(): lax.dynamic_slice(out_weight, ((f ^ bit) * block, 0), (block, channels))  5.7 us
    dot_general x1, matrix products, local_four(): jnp.dot(first, first_weight, preferred_element_type=jnp.float32)  3.94 us
    unnamed x40, local copies, waits for them, and re-layouts  3.82 us
  transfers between devices with their start and end apart: 15, of which 2 were waited for; matrix products, arithmetic and copies ran while one was open for 15% of the time, Pallas kernels for 21%

profile of v1, /device:TPU:0, one launch (start us, length us, event | category | flops | bytes accessed | tf_op | source)
XLA Modules:
  0.0 140.6 jit_solution(14802700801062054525)
XLA Ops:
  0.0 3.1 %constant_dynamic-slice_fusion.8 = (bf16[2048,256]{1,0:T(8,128)(2,1)}, bf16[2048,256]{1,0:T(8,128)(2,1)}) fusion(bf16[2048,1536]{1,0:T(8,128)(2,1)} %param.8, s32[]{:T(128)S(6)} %select_n.67, s32[]{:T(128)S(6)} %select_n.66), kind=kLoop, calls=%fused_computation.36 | loop fusion | bytes 4194312 | tf_op jit(solution)/shard_map/dynamic_slice | solution.py:260
  3.1 2.9 %collective-permute-start = (bf16[2048,256]{1,0:T(8,128)(2,1)}, bf16[2048,256]{1,0:T(8,128)(2,1)S(1)}, u32[]{:S(2)}, u32[]{:S(2)}) collective-permute-start(bf16[2048,256]{1,0:T(8,128)(2,1)} %get-tuple-element.13), channel_id=1, source_target_pairs={{0,8},{8,0},{16,24},{24,16},{1,9},{9,1},{17,25},{25,17},{2,10},{10... | collective-permute-start | bytes 3145736 | tf_op jit(solution)/shard_map/ppermute | solution.py:236
  6.1 1.5 %collective-permute-start.2 = (bf16[2048,256]{1,0:T(8,128)(2,1)}, bf16[2048,256]{1,0:T(8,128)(2,1)}, u32[]{:S(2)}, u32[]{:S(2)}) collective-permute-start(bf16[2048,256]{1,0:T(8,128)(2,1)} %get-tuple-element.12), channel_id=1, source_target_pairs={{0,16},{8,24},{16,0},{24,8},{1,17},{9,25},{17,1},{25,9},{2,18},{10... | collective-permute-start | bytes 3145736 | tf_op jit(solution)/shard_map/ppermute | solution.py:236
  8.1 47.2 %all-gather = s32[4,1,4]{2,1,0:T(1,128)S(1)} all-gather(s32[1,1,4]{2,1,0:T(1,128)S(1)} %bitcast.24), channel_id=1, replica_groups=mesh['fsdp'=4,'seq'=8] {'fsdp'}, dimensions={0}, use_global_device_ids=true | all-gather | bytes 80 | tf_op jit(solution)/shard_map/all_gather | solution.py:270
  55.5 3.1 %constant_dynamic-slice_fusion.10.own_ref = bf16[2048,512]{1,0:T(8,128)(2,1)} fusion(bf16[2048,1536]{1,0:T(8,128)(2,1)} %param.8, s32[]{:T(128)S(6)} %select_n.64), kind=kLoop, calls=%fused_computation.38 | loop fusion | bytes 4194308 | tf_op jit(solution)/shard_map/dynamic_slice | solution.py:258
  60.7 1.7 %collective-permute-start.11 = (bf16[128,2048]{1,0:T(8,128)(2,1)}, bf16[128,2048]{1,0:T(8,128)(2,1)}, u32[]{:S(2)}, u32[]{:S(2)}) collective-permute-start(bf16[128,2048]{1,0:T(8,128)(2,1)} %slice.27), channel_id=1, source_target_pairs={{0,16},{8,24},{16,0},{24,8},{1,17},{9,25},{17,1},{25,9},{2,18},{10... | collective-permute-start | bytes 1572872 | tf_op jit(solution)/shard_map/ppermute | solution.py:236
  68.3 5.7 %constant_dynamic-slice_fusion.3 = (bf16[512,2048]{1,0:T(8,128)(2,1)}, bf16[512,2048]{1,0:T(8,128)(2,1)}, bf16[512,2048]{1,0:T(8,128)(2,1)}) fusion(bf16[2048,2048]{1,0:T(8,128)(2,1)} %param.11, s32[]{:T(128)S(6)} %select_n.73, s32[]{:T(128)S(6)} %select_n.74, s32[]{:T(128)S(6)} %select_n.75), kind=kLoop, calls=%fused_computation.31 | loop fusion | bytes 12582924 | tf_op jit(solution)/shard_map/dynamic_slice | solution.py:291
  74.9 2.4 %collective-permute-done.12 = bf16[128,2048]{1,0:T(8,128)(2,1)} collective-permute-done((bf16[128,2048]{1,0:T(8,128)(2,1)}, bf16[128,2048]{1,0:T(8,128)(2,1)}, u32[]{:S(2)}, u32[]{:S(2)}) %collective-permute-start.12) | collective-permute-done | bytes 524320 | tf_op jit(solution)/shard_map/ppermute | solution.py:236
  78.6 4.0 %shard_map.64.proj_ref = bf16[3,256,512]{2,1,0:T(8,128)(2,1)S(1)} custom-call(bf16[256,2048]{1,0:T(8,128)(2,1)} %tok_ref.1, bf16[2048,512]{1,0:T(8,128)(2,1)S(1)} %copy-done.1, bf16[2048,256]{1,0:T(8,128)(2,1)S(1)} %collective-permute-done.xm_ref, bf16[2048,256]{1,0:T(8,128)(2,1)} %collective-permute-done.1.xo_ref, ...), custom_call_target="tpu_custom_call" | custom-call | flops 1610612736 | bytes 8126464 | tf_op jit(solution)/shard_map/pallas_call | solution.py:126
  84.3 2.2 %collective-permute-start.4 = (bf16[3,144,512]{2,1,0:T(8,128)(2,1)}, bf16[3,144,512]{2,1,0:T(8,128)(2,1)}, u32[]{:S(2)}, u32[]{:S(2)}) collective-permute-start(bf16[3,144,512]{2,1,0:T(8,128)(2,1)} %slice.24), channel_id=1, source_target_pairs={{0,1},{1,2},{2,3},{3,4},{4,5},{5,6},{6,7},{8,9},{9,10},{10,11},{11... | collective-permute-start | bytes 1327112 | tf_op jit(solution)/shard_map/ppermute | solution.py:14
  86.5 3.6 %shard_map.71.proj_ref = bf16[3,256,512]{2,1,0:T(8,128)(2,1)S(1)} custom-call(bf16[256,2048]{1,0:T(8,128)(2,1)S(1)} %pad_maximum_fusion.tok_ref, bf16[2048,512]{1,0:T(8,128)(2,1)S(1)} %copy-done.1, bf16[2048,256]{1,0:T(8,128)(2,1)S(1)} %collective-permute-done.xm_ref, bf16[2048,256]{1,0:T(8,128)(2,1)} %collective-permute-done.1.xo_ref, ...), custom_call_target="tpu_custom_call" | custom-call | flops 1610612736 | bytes 8126464 | tf_op jit(solution)/shard_map/pallas_call | solution.py:126
  91.2 4.4 %collective-permute-start.13 = (bf16[3,144,512]{2,1,0:T(8,128)(2,1)}, bf16[3,144,512]{2,1,0:T(8,128)(2,1)}, u32[]{:S(2)}, u32[]{:S(2)}) collective-permute-start(bf16[3,144,512]{2,1,0:T(8,128)(2,1)} %slice.29), channel_id=1, source_target_pairs={{0,1},{1,2},{2,3},{3,4},{4,5},{5,6},{6,7},{8,9},{9,10},{10,11},{11... | collective-permute-start | bytes 1327112 | tf_op jit(solution)/shard_map/ppermute | solution.py:14
  95.6 3.6 %shard_map.67.proj_ref = bf16[3,256,512]{2,1,0:T(8,128)(2,1)S(1)} custom-call(bf16[256,2048]{1,0:T(8,128)(2,1)S(1)} %copy-done.13, bf16[2048,512]{1,0:T(8,128)(2,1)S(1)} %copy-done.1, bf16[2048,256]{1,0:T(8,128)(2,1)S(1)} %collective-permute-done.xm_ref, bf16[2048,256]{1,0:T(8,128)(2,1)} %collective-permute-done.1.xo_ref, ...), custom_call_target="tpu_custom_call" | custom-call | flops 1610612736 | bytes 8126464 | tf_op jit(solution)/shard_map/pallas_call | solution.py:126
  100.3 2.1 %collective-permute-start.6 = (bf16[3,144,512]{2,1,0:T(8,128)(2,1)}, bf16[3,144,512]{2,1,0:T(8,128)(2,1)}, u32[]{:S(2)}, u32[]{:S(2)}) collective-permute-start(bf16[3,144,512]{2,1,0:T(8,128)(2,1)} %slice.25), channel_id=1, source_target_pairs={{0,1},{1,2},{2,3},{3,4},{4,5},{5,6},{6,7},{8,9},{9,10},{10,11},{11... | collective-permute-start | bytes 1327112 | tf_op jit(solution)/shard_map/ppermute | solution.py:14
  102.4 3.6 %shard_map.69.proj_ref = bf16[3,256,512]{2,1,0:T(8,128)(2,1)S(1)} custom-call(bf16[256,2048]{1,0:T(8,128)(2,1)S(1)} %copy-done.11, bf16[2048,512]{1,0:T(8,128)(2,1)S(1)} %copy-done.1, bf16[2048,256]{1,0:T(8,128)(2,1)S(1)} %collective-permute-done.xm_ref, bf16[2048,256]{1,0:T(8,128)(2,1)} %collective-permute-done.1.xo_ref, ...), custom_call_target="tpu_custom_call" | custom-call | flops 1610612736 | bytes 8126464 | tf_op jit(solution)/shard_map/pallas_call | solution.py:126
  107.7 2.9 %collective-permute-start.9 = (bf16[3,144,512]{2,1,0:T(8,128)(2,1)}, bf16[3,144,512]{2,1,0:T(8,128)(2,1)S(1)}, u32[]{:S(2)}, u32[]{:S(2)}) collective-permute-start(bf16[3,144,512]{2,1,0:T(8,128)(2,1)} %slice.26), channel_id=1, source_target_pairs={{0,1},{1,2},{2,3},{3,4},{4,5},{5,6},{6,7},{8,9},{9,10},{10,11},{11... | collective-permute-start | bytes 1327112 | tf_op jit(solution)/shard_map/ppermute | solution.py:14
  112.0 4.6 %shard_map.72 = bf16[256,512]{1,0:T(8,128)(2,1)S(1)} custom-call(s32[384,1]{1,0:T(8,128)S(1)} %reshape_subtract_fusion.pos_ref, bf16[3,144,512]{2,1,0:T(8,128)(2,1)} %collective-permute-done.13.halo_ref, bf16[3,256,512]{2,1,0:T(8,128)(2,1)S(1)} %copy-done.9, f32[3,7,512]{2,1,0:T(8,128)S(1)} %bitcast.17, bf16[4096,256]{1,0:T(8,128)(2,1)S(1)} %shard_map.65.table_ref), custom_call_target="tpu_custom_call" | custom-call | flops 536870912 | bytes 5685248 | tf_op jit(solution)/shard_map/pallas_call | solution.py:216
  116.7 1.5 %collective-permute-start.14 = (bf16[256,512]{1,0:T(8,128)(2,1)S(1)}, bf16[256,512]{1,0:T(8,128)(2,1)S(1)}, u32[]{:S(2)}, u32[]{:S(2)}) collective-permute-start(bf16[256,512]{1,0:T(8,128)(2,1)S(1)} %shard_map.72), channel_id=1, source_target_pairs={{0,24},{8,16},{16,8},{24,0},{1,25},{9,17},{17,9},{25,1},{2,26},{10... | collective-permute-start | bytes 786440 | tf_op jit(solution)/shard_map/ppermute | solution.py:236
  118.3 4.6 %shard_map.68 = bf16[256,512]{1,0:T(8,128)(2,1)S(1)} custom-call(s32[384,1]{1,0:T(8,128)S(1)} %copy-done.14, bf16[3,144,512]{2,1,0:T(8,128)(2,1)} %collective-permute-done.6.halo_ref, bf16[3,256,512]{2,1,0:T(8,128)(2,1)S(1)} %copy-done.7, f32[3,7,512]{2,1,0:T(8,128)S(1)} %bitcast.18, bf16[4096,256]{1,0:T(8,128)(2,1)S(1)} %shard_map.65.table_ref), custom_call_target="tpu_custom_call" | custom-call | flops 536870912 | bytes 5685248 | tf_op jit(solution)/shard_map/pallas_call | solution.py:216
  123.6 3.6 %shard_map.70 = bf16[256,512]{1,0:T(8,128)(2,1)S(1)} custom-call(s32[384,1]{1,0:T(8,128)S(1)} %reshape_subtract_fusion.1.pos_ref, bf16[3,144,512]{2,1,0:T(8,128)(2,1)S(1)} %collective-permute-done.9.halo_ref, bf16[3,256,512]{2,1,0:T(8,128)(2,1)S(1)} %copy-done.5, f32[3,7,512]{2,1,0:T(8,128)S(1)} %bitcast.19, bf16[4096,256]{1,0:T(8,128)(2,1)S(1)} %shard_map.65.table_ref), custom_call_target="tpu_custom_call" | custom-call | flops 536870912 | bytes 5685248 | tf_op jit(solution)/shard_map/pallas_call | solution.py:216
  127.2 1.6 %collective-permute-start.10 = (bf16[256,512]{1,0:T(8,128)(2,1)S(1)}, bf16[256,512]{1,0:T(8,128)(2,1)S(1)}, u32[]{:S(2)}, u32[]{:S(2)}) collective-permute-start(bf16[256,512]{1,0:T(8,128)(2,1)S(1)} %shard_map.70), channel_id=1, source_target_pairs={{0,16},{8,24},{16,0},{24,8},{1,17},{9,25},{17,1},{25,9},{2,18},{10... | collective-permute-start | bytes 786440 | tf_op jit(solution)/shard_map/ppermute | solution.py:236
  128.8 5.0 %shard_map.66 = bf16[256,512]{1,0:T(8,128)(2,1)S(1)} custom-call(s32[384,1]{1,0:T(8,128)S(1)} %reshape_subtract_fusion.3.pos_ref, bf16[3,144,512]{2,1,0:T(8,128)(2,1)} %collective-permute-done.4.halo_ref, bf16[3,256,512]{2,1,0:T(8,128)(2,1)S(1)} %copy-done.3, f32[3,7,512]{2,1,0:T(8,128)S(1)} %bitcast.20, bf16[4096,256]{1,0:T(8,128)(2,1)S(1)} %shard_map.65.table_ref), custom_call_target="tpu_custom_call" | custom-call | flops 536870912 | bytes 5685248 | tf_op jit(solution)/shard_map/pallas_call | solution.py:216
  133.8 2.5 %fusion.15 = f32[256,2048]{1,0:T(8,128)S(1)} fusion(bf16[256,512]{1,0:T(8,128)(2,1)S(1)} %collective-permute-done.14, bf16[2048,2048]{1,0:T(8,128)(2,1)} %param.11, s32[]{:T(128)S(6)} %select_n.78), kind=kOutput, calls=%fused_computation.9 | convolution fusion | flops 536870912 | bytes 4456452 | tf_op jit(solution)/shard_map/dot_general | solution.py:298
  136.6 3.9 %fusion.12 = bf16[256,2048]{1,0:T(8,128)(2,1)} fusion(f32[256,2048]{1,0:T(8,128)S(1)} %fusion.15, bf16[512,2048]{1,0:T(8,128)(2,1)S(1)} %copy-done.17, bf16[512,2048]{1,0:T(8,128)(2,1)S(1)} %copy-done.16, bf16[512,2048]{1,0:T(8,128)(2,1)S(1)} %copy-done.15, bf16[256,2048]{1,0:T(8,128)(2,1)} %tok_ref.1, bf16[256,512]{1,0:T(8,128)(2,1)S(1)} %collective-permute-done.10, ...), kind=kOutput, calls=%fused_computation.8 | convolution fusion | flops 1633943552 | bytes 11272192 | tf_op jit(solution)/shard_map/dot_general | solution.py:295
  (82 shorter events, 18.9 us)
Async XLA Ops:
  0.0 64.9 %copy-start = (bf16[128,128]{1,0:T(8,128)(2,1)S(1)}, bf16[128,128]{1,0:T(8,128)(2,1)}, u32[]{:S(2)}) copy-start(bf16[128,128]{1,0:T(8,128)(2,1)} %param.10) | copy-start | bytes 98308
  0.0 8.1 %copy-start.18 = (s32[1,4]{1,0:T(1,128)S(1)}, s32[1,4]{1,0:T(1,128)}, u32[]{:S(2)}) copy-start(s32[1,4]{1,0:T(1,128)} %param.7) | copy-start | bytes 52
  3.1 55.4 %collective-permute-start = (bf16[2048,256]{1,0:T(8,128)(2,1)}, bf16[2048,256]{1,0:T(8,128)(2,1)S(1)}, u32[]{:S(2)}, u32[]{:S(2)}) collective-permute-start(bf16[2048,256]{1,0:T(8,128)(2,1)} %get-tuple-element.13), channel_id=1, source_target_pairs={{0,8},{8,0},{16,24},{24,16},{1,9},{9,1},{17,25},{25,17},{2,10},{10... | collective-permute-start | bytes 3145736 | tf_op jit(solution)/shard_map/ppermute | solution.py:236
  6.1 52.5 %collective-permute-start.2 = (bf16[2048,256]{1,0:T(8,128)(2,1)}, bf16[2048,256]{1,0:T(8,128)(2,1)}, u32[]{:S(2)}, u32[]{:S(2)}) collective-permute-start(bf16[2048,256]{1,0:T(8,128)(2,1)} %get-tuple-element.12), channel_id=1, source_target_pairs={{0,16},{8,24},{16,0},{24,8},{1,17},{9,25},{17,1},{25,9},{2,18},{10... | collective-permute-start | bytes 3145736 | tf_op jit(solution)/shard_map/ppermute | solution.py:236
  7.6 52.2 %collective-permute-start.5 = (bf16[256,2048]{1,0:T(8,128)(2,1)}, bf16[256,2048]{1,0:T(8,128)(2,1)S(1)}, u32[]{:S(2)}, u32[]{:S(2)}) collective-permute-start(bf16[256,2048]{1,0:T(8,128)(2,1)} %tok_ref.1), channel_id=1, source_target_pairs={{0,8},{8,0},{16,24},{24,16},{1,9},{9,1},{17,25},{25,17},{2,10},{10... | collective-permute-start | bytes 3145736 | tf_op jit(solution)/shard_map/ppermute | solution.py:236
  8.1 54.4 %collective-permute-start.8 = (bf16[256,2048]{1,0:T(8,128)(2,1)}, bf16[256,2048]{1,0:T(8,128)(2,1)S(1)}, u32[]{:S(2)}, u32[]{:S(2)}) collective-permute-start(bf16[256,2048]{1,0:T(8,128)(2,1)} %tok_ref.1), channel_id=1, source_target_pairs={{0,16},{8,24},{16,0},{24,8},{1,17},{9,25},{17,1},{25,9},{2,18},{10... | collective-permute-start | bytes 3145736 | tf_op jit(solution)/shard_map/ppermute | solution.py:236
  58.6 20.1 %collective-permute-start.1 = (bf16[2048,256]{1,0:T(8,128)(2,1)S(1)}, bf16[2048,256]{1,0:T(8,128)(2,1)}, u32[]{:S(2)}, u32[]{:S(2)}) collective-permute-start(bf16[2048,256]{1,0:T(8,128)(2,1)S(1)} %collective-permute-done.xm_ref), channel_id=1, source_target_pairs={{0,1},{1,0},{2,3},{3,2},{4,5},{5,4},{6,7},{7,6},{8,9},{9,8},{10,11... | collective-permute-start | bytes 3145736 | tf_op jit(solution)/shard_map/ppermute | solution.py:240
  58.6 20.1 %collective-permute-start.3 = (bf16[2048,256]{1,0:T(8,128)(2,1)}, bf16[2048,256]{1,0:T(8,128)(2,1)}, u32[]{:S(2)}, u32[]{:S(2)}) collective-permute-start(bf16[2048,256]{1,0:T(8,128)(2,1)} %collective-permute-done.2.ym_ref), channel_id=1, source_target_pairs={{0,1},{1,0},{2,3},{3,2},{4,5},{5,4},{6,7},{7,6},{8,9},{9,8},{10,11... | collective-permute-start | bytes 3145736 | tf_op jit(solution)/shard_map/ppermute | solution.py:240
  60.7 14.2 %collective-permute-start.11 = (bf16[128,2048]{1,0:T(8,128)(2,1)}, bf16[128,2048]{1,0:T(8,128)(2,1)}, u32[]{:S(2)}, u32[]{:S(2)}) collective-permute-start(bf16[128,2048]{1,0:T(8,128)(2,1)} %slice.27), channel_id=1, source_target_pairs={{0,16},{8,24},{16,0},{24,8},{1,17},{9,25},{17,1},{25,9},{2,18},{10... | collective-permute-start | bytes 1572872 | tf_op jit(solution)/shard_map/ppermute | solution.py:236
  63.4 13.9 %collective-permute-start.12 = (bf16[128,2048]{1,0:T(8,128)(2,1)}, bf16[128,2048]{1,0:T(8,128)(2,1)}, u32[]{:S(2)}, u32[]{:S(2)}) collective-permute-start(bf16[128,2048]{1,0:T(8,128)(2,1)} %slice.28), channel_id=1, source_target_pairs={{0,8},{8,0},{16,24},{24,16},{1,9},{9,1},{17,25},{25,17},{2,10},{10... | collective-permute-start | bytes 1572872 | tf_op jit(solution)/shard_map/ppermute | solution.py:236
  84.3 11.3 %copy-start.13 = (bf16[256,2048]{1,0:T(8,128)(2,1)S(1)}, bf16[256,2048]{1,0:T(8,128)(2,1)}, u32[]{:S(2)}) copy-start(bf16[256,2048]{1,0:T(8,128)(2,1)} %copy-done.12) | copy-start | bytes 3145732
  84.3 44.5 %collective-permute-start.4 = (bf16[3,144,512]{2,1,0:T(8,128)(2,1)}, bf16[3,144,512]{2,1,0:T(8,128)(2,1)}, u32[]{:S(2)}, u32[]{:S(2)}) collective-permute-start(bf16[3,144,512]{2,1,0:T(8,128)(2,1)} %slice.24), channel_id=1, source_target_pairs={{0,1},{1,2},{2,3},{3,4},{4,5},{5,6},{6,7},{8,9},{9,10},{10,11},{11... | collective-permute-start | bytes 1327112 | tf_op jit(solution)/shard_map/ppermute | solution.py:14
  91.2 11.2 %copy-start.11 = (bf16[256,2048]{1,0:T(8,128)(2,1)S(1)}, bf16[256,2048]{1,0:T(8,128)(2,1)}, u32[]{:S(2)}) copy-start(bf16[256,2048]{1,0:T(8,128)(2,1)} %copy-done.10) | copy-start | bytes 3145732
  91.2 19.6 %collective-permute-start.13 = (bf16[3,144,512]{2,1,0:T(8,128)(2,1)}, bf16[3,144,512]{2,1,0:T(8,128)(2,1)}, u32[]{:S(2)}, u32[]{:S(2)}) collective-permute-start(bf16[3,144,512]{2,1,0:T(8,128)(2,1)} %slice.29), channel_id=1, source_target_pairs={{0,1},{1,2},{2,3},{3,4},{4,5},{5,6},{6,7},{8,9},{9,10},{10,11},{11... | collective-permute-start | bytes 1327112 | tf_op jit(solution)/shard_map/ppermute | solution.py:14
  100.3 18.0 %collective-permute-start.6 = (bf16[3,144,512]{2,1,0:T(8,128)(2,1)}, bf16[3,144,512]{2,1,0:T(8,128)(2,1)}, u32[]{:S(2)}, u32[]{:S(2)}) collective-permute-start(bf16[3,144,512]{2,1,0:T(8,128)(2,1)} %slice.25), channel_id=1, source_target_pairs={{0,1},{1,2},{2,3},{3,4},{4,5},{5,6},{6,7},{8,9},{9,10},{10,11},{11... | collective-permute-start | bytes 1327112 | tf_op jit(solution)/shard_map/ppermute | solution.py:14
  107.7 15.9 %collective-permute-start.9 = (bf16[3,144,512]{2,1,0:T(8,128)(2,1)}, bf16[3,144,512]{2,1,0:T(8,128)(2,1)S(1)}, u32[]{:S(2)}, u32[]{:S(2)}) collective-permute-start(bf16[3,144,512]{2,1,0:T(8,128)(2,1)} %slice.26), channel_id=1, source_target_pairs={{0,1},{1,2},{2,3},{3,4},{4,5},{5,6},{6,7},{8,9},{9,10},{10,11},{11... | collective-permute-start | bytes 1327112 | tf_op jit(solution)/shard_map/ppermute | solution.py:14
  110.7 7.6 %copy-start.7 = (bf16[3,256,512]{2,1,0:T(8,128)(2,1)S(1)}, bf16[3,256,512]{2,1,0:T(8,128)(2,1)}, u32[]{:S(2)}) copy-start(bf16[3,256,512]{2,1,0:T(8,128)(2,1)} %copy-done.6) | copy-start | bytes 2359300
  112.0 6.3 %copy-start.14 = (s32[384,1]{1,0:T(8,128)S(1)}, s32[384,1]{1,0:T(8,128)}, u32[]{:S(2)}) copy-start(s32[384,1]{1,0:T(8,128)} %reshape_subtract_fusion.2.pos_ref) | copy-start | bytes 4612
  116.7 6.9 %copy-start.5 = (bf16[3,256,512]{2,1,0:T(8,128)(2,1)S(1)}, bf16[3,256,512]{2,1,0:T(8,128)(2,1)}, u32[]{:S(2)}) copy-start(bf16[3,256,512]{2,1,0:T(8,128)(2,1)} %copy-done.4) | copy-start | bytes 2359300
  116.7 17.1 %collective-permute-start.14 = (bf16[256,512]{1,0:T(8,128)(2,1)S(1)}, bf16[256,512]{1,0:T(8,128)(2,1)S(1)}, u32[]{:S(2)}, u32[]{:S(2)}) collective-permute-start(bf16[256,512]{1,0:T(8,128)(2,1)S(1)} %shard_map.72), channel_id=1, source_target_pairs={{0,24},{8,16},{16,8},{24,0},{1,25},{9,17},{17,9},{25,1},{2,26},{10... | collective-permute-start | bytes 786440 | tf_op jit(solution)/shard_map/ppermute | solution.py:236
  123.0 5.8 %copy-start.3 = (bf16[3,256,512]{2,1,0:T(8,128)(2,1)S(1)}, bf16[3,256,512]{2,1,0:T(8,128)(2,1)}, u32[]{:S(2)}) copy-start(bf16[3,256,512]{2,1,0:T(8,128)(2,1)} %copy-done.2) | copy-start | bytes 2359300
  123.0 13.3 %collective-permute-start.7 = (bf16[256,512]{1,0:T(8,128)(2,1)S(1)}, bf16[256,512]{1,0:T(8,128)(2,1)S(1)}, u32[]{:S(2)}, u32[]{:S(2)}) collective-permute-start(bf16[256,512]{1,0:T(8,128)(2,1)S(1)} %shard_map.68), channel_id=1, source_target_pairs={{0,8},{8,0},{16,24},{24,16},{1,9},{9,1},{17,25},{25,17},{2,10},{10... | collective-permute-start | bytes 786440 | tf_op jit(solution)/shard_map/ppermute | solution.py:236
  127.2 9.1 %collective-permute-start.10 = (bf16[256,512]{1,0:T(8,128)(2,1)S(1)}, bf16[256,512]{1,0:T(8,128)(2,1)S(1)}, u32[]{:S(2)}, u32[]{:S(2)}) collective-permute-start(bf16[256,512]{1,0:T(8,128)(2,1)S(1)} %shard_map.70), channel_id=1, source_target_pairs={{0,16},{8,24},{16,0},{24,8},{1,17},{9,25},{17,1},{25,9},{2,18},{10... | collective-permute-start | bytes 786440 | tf_op jit(solution)/shard_map/ppermute | solution.py:236
  128.8 7.5 %copy-start.17 = (bf16[512,2048]{1,0:T(8,128)(2,1)S(1)}, bf16[512,2048]{1,0:T(8,128)(2,1)}, u32[]{:S(2)}) copy-start(bf16[512,2048]{1,0:T(8,128)(2,1)} %get-tuple-element.11) | copy-start | bytes 6291460
  (10 other events, 23.0 us)

commit v2 on v1

--- a/solution.py
+++ b/solution.py
@@ -97,20 +97,25 @@
     return result.astype(jnp.bfloat16)
 
 
-def role_kernel(tok_ref, own_ref, xm_ref, xo_ref, ym_ref, yo_ref, out_ref):
+def role_kernel(n, *refs):
+    toks, weights, out_ref, tail_ref = refs[: 2 * n], refs[2 * n : -2], refs[-2], refs[-1]
+    own_ref, xm_ref, xo_ref, ym_ref, yo_ref = weights
     f = lax.axis_index("fsdp")
     core = lax.rem(lax.axis_index("seq"), 2)
     half = xm_ref.shape[1]
     own_role = jnp.where(f == 0, 0, jnp.where(f == 3, 2, 1))
     x_role = jnp.where(f == 1, 0, jnp.where(f == 2, 2, 1))
     y_role = jnp.where(f < 2, 2, 0)
-    tok = tok_ref[...]
+    rows = out_ref.shape[2]
+    tok = jnp.concatenate([ref[...] for ref in toks], axis=0)
+    tail = tail_ref.shape[2]
 
     def put(role, column, weight):
         columns = pl.ds(pl.multiple_of(column, half), half)
-        out_ref[role, :, columns] = jnp.dot(
-            tok, weight, preferred_element_type=jnp.float32
-        ).astype(jnp.bfloat16)
+        made = jnp.dot(tok, weight, preferred_element_type=jnp.float32).astype(jnp.bfloat16)
+        for p in range(n):
+            out_ref[p, role, :, columns] = made[p * rows : (p + 1) * rows]
+            tail_ref[p, role, :, columns] = made[(p + 1) * rows - tail : (p + 1) * rows]
 
     put(own_role, 0, own_ref[:, :half])
     put(own_role, half, own_ref[:, half:])
@@ -121,20 +126,25 @@
     put(y_role, other, yo_ref[...])
 
 
-def project(tok, blocks):
-    rows, block = tok.shape[0], blocks[0].shape[1]
+def project(toks, blocks, tail):
+    n = len(toks) // 2
+    rows, block = 2 * toks[0].shape[0], blocks[0].shape[1]
+    depth = toks[0].shape[1]
     return pl.pallas_call(
-        role_kernel,
-        out_shape=jax.ShapeDtypeStruct((3, rows, block), jnp.bfloat16),
-        in_specs=[pl.BlockSpec(memory_space=pltpu.VMEM)] * 6,
-        out_specs=pl.BlockSpec(memory_space=pltpu.VMEM),
+        functools.partial(role_kernel, n),
+        out_shape=[
+            jax.ShapeDtypeStruct((n, 3, rows, block), jnp.bfloat16),
+            jax.ShapeDtypeStruct((n, 3, tail, block), jnp.bfloat16),
+        ],
+        in_specs=[pl.BlockSpec(memory_space=pltpu.VMEM)] * (2 * n + 5),
+        out_specs=[pl.BlockSpec(memory_space=pltpu.VMEM)] * 2,
         compiler_params=pltpu.CompilerParams(vmem_limit_bytes=40 << 20),
         cost_estimate=pl.CostEstimate(
-            flops=2 * rows * tok.shape[1] * 3 * block,
-            bytes_accessed=2 * (tok.size + 3 * tok.shape[1] * block + 3 * rows * block),
+            flops=2 * n * rows * depth * 3 * block,
+            bytes_accessed=2 * (n * rows * depth + 3 * depth * block + 5 * n * rows * block),
             transcendentals=0,
         ),
-    )(tok, *blocks)
+    )(*toks, *blocks)
 
 
 def table_kernel(taps_ref, table_ref):
@@ -157,8 +167,15 @@
     )(taps)
 
 
-def mix_kernel(width, per_group, pos_ref, halo_ref, proj_ref, taps_ref, table_ref, out_ref,
-               ext_ref, mixed_ref, query_ref):
+def mix_kernel(width, per_group, pos_all, halo_all, proj_all, taps_ref, table_ref, *refs):
+    count = pos_all.shape[0]
+    for p in range(count):
+        mix_pack(width, per_group, pos_all.at[p], halo_all.at[p], proj_all.at[p], taps_ref,
+                 table_ref, refs[p], *refs[count:])
+
+
+def mix_pack(width, per_group, pos_ref, halo_ref, proj_ref, taps_ref, table_ref, out_ref,
+             ext_ref, mixed_ref, query_ref):
     halo, rows, channels = halo_ref.shape[1], proj_ref.shape[1], proj_ref.shape[2]
     window = table_ref.shape[1]
     fl = window // 2
@@ -211,21 +228,21 @@
 
 
 def mix(pos, halo, proj, taps, table, width, per_group):
-    _, rows, channels = proj.shape
+    n, _, rows, channels = proj.shape
     fl = table.shape[1] // 2
     return pl.pallas_call(
         functools.partial(mix_kernel, width, per_group),
-        out_shape=jax.ShapeDtypeStruct((rows, channels), jnp.bfloat16),
+        out_shape=[jax.ShapeDtypeStruct((rows, channels), jnp.bfloat16)] * n,
         in_specs=[pl.BlockSpec(memory_space=pltpu.VMEM)] * 5,
-        out_specs=pl.BlockSpec(memory_space=pltpu.VMEM),
+        out_specs=[pl.BlockSpec(memory_space=pltpu.VMEM)] * n,
         scratch_shapes=[
-            pltpu.VMEM((3, halo.shape[1] + rows, channels), jnp.float32),
+            pltpu.VMEM((3, halo.shape[2] + rows, channels), jnp.float32),
             pltpu.VMEM((fl + rows, channels), jnp.bfloat16),
             pltpu.VMEM((rows, channels), jnp.float32),
         ],
         compiler_params=pltpu.CompilerParams(vmem_limit_bytes=40 << 20),
         cost_estimate=pl.CostEstimate(
-            flops=4 * rows * table.size // 2,
+            flops=2 * n * rows * table.size,
             bytes_accessed=2 * (table.size + halo.size + 4 * proj.size),
             transcendentals=0,
         ),
@@ -252,8 +269,6 @@
     half = block // 2
     groups = group_count // 4
 
-    tok_x = swap(tokens, 1)
-    tok_y = swap(tokens, 2)
     odd = f % 2
     own = lax.dynamic_slice(in_weight, (0, odd * 2 * block), (channels, block))
     x_send = lax.dynamic_slice(in_weight, (0, block + core * half), (channels, half))
@@ -262,13 +277,14 @@
     y_mine = swap(y_send, 2)
     x_other = swap_cores(x_mine)
     y_other = swap_cores(y_mine)
-    tok_d = jnp.concatenate(
-        [swap(tok_x[: rows // 2], 2), swap(tok_y[rows // 2 :], 1)], axis=0
-    )
+    low, high = tokens[: rows // 2], tokens[rows // 2 :]
+    to_x = lax.optimization_barrier((low, high, x_mine))
+    to_y = lax.optimization_barrier((high, low, y_mine))
+    x_low, y_high = swap(to_x[0], 1), swap(to_y[0], 2)
+    x_high, y_low = swap(to_x[1], 1), swap(to_y[1], 2)
     blocks = (own, x_mine, x_other, y_mine, y_other)
 
-    lengths = lax.all_gather(seq_lengths, "fsdp", axis=0, tiled=True)
-    seq_starts = jnp.cumsum(lengths, axis=1) - lengths
+    lengths = [seq_lengths[0]] + [swap(seq_lengths, bit)[0] for bit in (1, 2, 3)]
     row_ids = seq * rows - filter_len + jnp.arange(rows + filter_len, dtype=jnp.int32)
     taps = lax.dynamic_slice(
         short_filter.reshape(width, 3, 4, block), (0, 0, f, 0), (width, 3, 1, block)
@@ -278,20 +294,36 @@
     table = toeplitz(jnp.pad(reverse, ((0, 0), (1, filter_len - 1))))
 
     halo_rows = filter_len + 16
-    gated = []
-    for bit, tok in ((0, tokens), (1, tok_x), (2, tok_y), (3, tok_d)):
-        proj = project(tok, blocks)
-        halo = from_behind(proj[:, rows - halo_rows :], "seq", 1)
-        starts = lax.dynamic_slice(seq_starts, (f ^ bit, 0), (1, seq_starts.shape[1]))[0]
-        pos = positions(row_ids, starts)[:, None]
-        out = mix(pos, halo, proj, taps, table, width, per_group)
-        gated.append(out if bit == 0 else swap(out, bit))
+
+    def position_of(bit):
+        return positions(row_ids, jnp.cumsum(lengths[bit]) - lengths[bit])[:, None]
+
+    def mix_packs(bits, proj, halo):
+        pos = jnp.stack([position_of(bit) for bit in bits])
+        return mix(pos, halo, proj, taps, table, width, per_group)
 
     def rows_of(bit):
         return lax.dynamic_slice(out_weight, ((f ^ bit) * block, 0), (block, channels))
 
+    proj_own, tail = project((low, high), blocks, halo_rows)
+    halo_own = from_behind(tail, "seq", 1)
+    to_d = lax.optimization_barrier((x_low, y_high, tail))
+    d_low, d_high = swap(to_d[0], 2), swap(to_d[1], 1)
+    (own_out,) = mix_packs((0,), proj_own, halo_own)
+    first_weight = jnp.concatenate([rows_of(0), rows_of(1), rows_of(2)], axis=0)
+    others = lax.optimization_barrier((x_low, x_high, y_low, y_high, own_out, first_weight))
+    first_weight = others[5]
+    proj_xy, tail_xy = project(others[:4], blocks, halo_rows)
+    halo_xy = from_behind(tail_xy, "seq", 1)
+    last = lax.optimization_barrier((d_low, d_high, tail_xy))
+    proj_d, tail_d = project(last[:2], blocks, halo_rows)
+    halo_d = from_behind(tail_d, "seq", 1)
+    x_out, y_out = mix_packs((1, 2), *lax.optimization_barrier((proj_xy, halo_xy, tail_d))[:2])
+    proj_d, halo_d, _ = lax.optimization_barrier((proj_d, halo_d, x_out))
+    (d_out,) = mix_packs((3,), proj_d, halo_d)
+    gated = [own_out, swap(x_out, 1), swap(y_out, 2), swap(d_out, 3)]
+
     first = jnp.concatenate(gated[:3], axis=1)
-    first_weight = jnp.concatenate([rows_of(0), rows_of(1), rows_of(2)], axis=0)
     result = tokens.astype(jnp.float32) + jnp.dot(
         first, first_weight, preferred_element_type=jnp.float32
     )

time: 141 us -> 126 us (0.89); the launches traced: 141 us -> 124 us
  blocking collectives: 47.2 us -> 0 us
  waiting for transfers between devices: 3.33 us -> 34.3 us
  other arithmetic: 3.86 us -> 16.1 us
  local copies, waits for them, and re-layouts: 22.2 us -> 15.4 us
  Pallas kernels: 33.3 us -> 28 us
  starting transfers between devices: 23.9 us -> 22.2 us
  matrix products: 6.39 us -> 7.87 us
    all_gather x1 -> x0, blocking collectives: 47.2 us -> none  [local_four(): lengths = lax.all_gather(seq_lengths, 'fsdp', axis=0, tiled=True)]
    ppermute x9 -> x14, waiting for transfers between devices: 3.32 us -> 34.3 us  [swap(): return lax.ppermute(block, 'fsdp', [(i, i ^ bit) for i in range(4)])]
    concatenate x1, other arithmetic: 1.3 us -> 11.2 us  [local_four(): first_weight = jnp.concatenate([rows_of(0), rows_of(1), rows_of(2)], axis=0)]
    ppermute x4 -> x3, starting transfers between devices: 11.5 us -> 4.38 us  [from_behind(): return lax.ppermute(block, axis, route)]
    ppermute x9 -> x14, starting transfers between devices: 11.9 us -> 17.8 us  [swap(): return lax.ppermute(block, 'fsdp', [(i, i ^ bit) for i in range(4)])]
    slice x6 -> x1, local copies, waits for them, and re-layouts: 5.15 us -> 1.12 us  [local_four(): low, high = (tokens[:rows // 2], tokens[rows // 2:])]
    pallas_call x4 -> x3, Pallas kernels: 17.8 us -> 14.7 us  [mix(): pl.pallas_call(functools.partial(mix_kernel, width, per_group), out_shape...]
    another operation x1 -> x5, other arithmetic: 0.18 us -> 2.52 us  [local_four(): seq_starts = jnp.cumsum(lengths, axis=1) - lengths]
  transfers between devices with their start and end apart: 15 -> 19, of which waited for: 2 -> 11; matrix products, arithmetic and copies ran while one was open for 15% -> 24% of each run, Pallas kernels for 21% -> 20%
where the time goes in v2:
time: 126 us; the launch traced here: 124 us
  waiting for transfers between devices  34.3 us (27%)
  Pallas kernels  28 us (22%)
  starting transfers between devices  22.2 us (18%)
  other arithmetic  16.1 us (13%)
  local copies, waits for them, and re-layouts  15.4 us (12%)
  matrix products  7.87 us (6%)
    ppermute x14, waiting for transfers between devices, swap(): return lax.ppermute(block, 'fsdp', [(i, i ^ bit) for i in range(4)])  34.3 us
    ppermute x14, starting transfers between devices, swap(): return lax.ppermute(block, 'fsdp', [(i, i ^ bit) for i in range(4)])  17.8 us
    pallas_call x3, Pallas kernels, mix(): pl.pallas_call(functools.partial(mix_kernel, width, per_group), out_shape...  14.7 us
    pallas_call x3, Pallas kernels, project(): pl.pallas_call(functools.partial(role_kernel, n), out_shape=[jax.ShapeDty...  12.6 us
    concatenate x1, other arithmetic, local_four(): first_weight = jnp.concatenate([rows_of(0), rows_of(1), rows_of(2)], axis=0)  11.2 us
    dot_general x1, matrix products, local_four(): jnp.dot(first, first_weight, preferred_element_type=jnp.float32)  5.57 us
    ppermute x3, starting transfers between devices, from_behind(): return lax.ppermute(block, axis, route)  4.38 us
    dynamic_slice x1, local copies, waits for them, and re-layouts, rows_of(): lax.dynamic_slice(out_weight, ((f ^ bit) * block, 0), (block, channels))  4.05 us
  transfers between devices with their start and end apart: 19, of which 11 were waited for; matrix products, arithmetic and copies ran while one was open for 24% of the time, Pallas kernels for 20%

profile of v2, /device:TPU:0, one launch (start us, length us, event | category | flops | bytes accessed | tf_op | source)
XLA Modules:
  0.0 124.1 jit_solution(5781452630937185034)
XLA Ops:
  0.0 3.9 %collective-permute-start.16 = (s32[1,4]{1,0:T(1,128)}, s32[1,4]{1,0:T(1,128)}, u32[]{:S(2)}, u32[]{:S(2)}) collective-permute-start(s32[1,4]{1,0:T(1,128)} %param.7), channel_id=1, source_target_pairs={{0,24},{8,16},{16,8},{24,0},{1,25},{9,17},{17,9},{25,1},{2,26},{10... | collective-permute-start | bytes 56 | tf_op jit(solution)/shard_map/ppermute | solution.py:253
  4.5 3.0 %constant_dynamic-slice_fusion.5 = (bf16[2048,256]{1,0:T(8,128)(2,1)}, bf16[2048,256]{1,0:T(8,128)(2,1)}) fusion(bf16[2048,1536]{1,0:T(8,128)(2,1)} %param.8, s32[]{:T(128)S(6)} %select_n.56, s32[]{:T(128)S(6)} %select_n.55), kind=kLoop, calls=%fused_computation.28 | loop fusion | bytes 4194312 | tf_op jit(solution)/shard_map/dynamic_slice | solution.py:275
  7.6 1.9 %collective-permute-start = (bf16[2048,256]{1,0:T(8,128)(2,1)}, bf16[2048,256]{1,0:T(8,128)(2,1)S(1)}, u32[]{:S(2)}, u32[]{:S(2)}) collective-permute-start(bf16[2048,256]{1,0:T(8,128)(2,1)} %get-tuple-element.63), channel_id=1, source_target_pairs={{0,8},{8,0},{16,24},{24,16},{1,9},{9,1},{17,25},{25,17},{2,10},{10... | collective-permute-start | bytes 3145736 | tf_op jit(solution)/shard_map/ppermute | solution.py:253
  11.7 3.1 %constant_dynamic-slice_fusion.7.refs_2_.refs_4_ = bf16[2048,512]{1,0:T(8,128)(2,1)} fusion(bf16[2048,1536]{1,0:T(8,128)(2,1)} %param.8, s32[]{:T(128)S(6)} %select_n.53), kind=kLoop, calls=%fused_computation.30 | loop fusion | bytes 4194308 | tf_op jit(solution)/shard_map/dynamic_slice | solution.py:273
  16.6 4.1 %constant_dynamic-slice_fusion.2 = (bf16[512,2048]{1,0:T(8,128)(2,1)S(1)}, bf16[512,2048]{1,0:T(8,128)(2,1)S(1)}, bf16[512,2048]{1,0:T(8,128)(2,1)S(1)}) fusion(bf16[2048,2048]{1,0:T(8,128)(2,1)} %param.11, s32[]{:T(128)S(6)} %select_n.61, s32[]{:T(128)S(6)} %select_n.62, s32[]{:T(128)S(6)} %select_n.63), kind=kLoop, calls=%fused_computation.25 | loop fusion | bytes 12582924 | tf_op jit(solution)/shard_map/dynamic_slice | solution.py:306
  21.8 10.3 %collective-permute-done.refs_3_.refs_5_ = bf16[2048,256]{1,0:T(8,128)(2,1)S(1)} collective-permute-done((bf16[2048,256]{1,0:T(8,128)(2,1)}, bf16[2048,256]{1,0:T(8,128)(2,1)S(1)}, u32[]{:S(2)}, u32[]{:S(2)}) %collective-permute-start) | collective-permute-done | bytes 1048608 | tf_op jit(solution)/shard_map/ppermute | solution.py:253
  33.6 11.2 %pad_maximum_fusion = bf16[1536,2048]{1,0:T(8,128)(2,1)} fusion(bf16[512,2048]{1,0:T(8,128)(2,1)S(1)} %get-tuple-element.61, bf16[512,2048]{1,0:T(8,128)(2,1)S(1)} %get-tuple-element.60, bf16[512,2048]{1,0:T(8,128)(2,1)S(1)} %get-tuple-element.59), kind=kLoop, calls=%fused_computation | loop fusion | flops 18874368 | bytes 12582912 | tf_op jit(solution)/shard_map/concatenate | solution.py:313
  51.8 1.6 %copy-done.1 = bf16[2048,512]{1,0:T(8,128)(2,1)S(1)} copy-done((bf16[2048,512]{1,0:T(8,128)(2,1)S(1)}, bf16[2048,512]{1,0:T(8,128)(2,1)}, u32[]{:S(2)}) %copy-start.1) | copy-done | bytes 2097176
  55.5 3.7 %shard_map.64 = (bf16[1,3,256,512]{3,2,1,0:T(8,128)(2,1)S(1)}, bf16[1,3,144,512]{3,2,1,0:T(8,128)(2,1)S(1)}) custom-call(bf16[128,2048]{1,0:T(8,128)(2,1)S(1)} %copy-done.4, bf16[128,2048]{1,0:T(8,128)(2,1)S(1)} %copy-done.3, bf16[2048,512]{1,0:T(8,128)(2,1)S(1)} %copy-done.1, bf16[2048,256]{1,0:T(8,128)(2,1)S(1)} %collective-permute-done.refs_3_.refs_5_, ...), custom_call_target="tpu_custom_call" | custom-call | flops 1610612736 | bytes 8650752 | tf_op jit(solution)/shard_map/pallas_call | solution.py:133
  60.9 1.8 %collective-permute-done.10.refs_3_ = bf16[128,2048]{1,0:T(8,128)(2,1)S(1)} collective-permute-done((bf16[128,2048]{1,0:T(8,128)(2,1)}, bf16[128,2048]{1,0:T(8,128)(2,1)S(1)}, u32[]{:S(2)}, u32[]{:S(2)}) %collective-permute-start.10) | collective-permute-done | bytes 524320 | tf_op jit(solution)/shard_map/ppermute | solution.py:253
  62.6 2.1 %collective-permute-done.7.refs_0_ = bf16[128,2048]{1,0:T(8,128)(2,1)S(1)} collective-permute-done((bf16[128,2048]{1,0:T(8,128)(2,1)}, bf16[128,2048]{1,0:T(8,128)(2,1)S(1)}, u32[]{:S(2)}, u32[]{:S(2)}) %collective-permute-start.7) | collective-permute-done | bytes 524320 | tf_op jit(solution)/shard_map/ppermute | solution.py:253
  67.0 3.6 %shard_map.66 = bf16[256,512]{1,0:T(8,128)(2,1)S(1)} custom-call(s32[1,384,1]{2,1,0:T(8,128)S(1)} %reshape_subtract_fusion.3.pos_all, bf16[1,3,144,512]{3,2,1,0:T(8,128)(2,1)S(1)} %collective-permute-done.4.halo_all, bf16[1,3,256,512]{3,2,1,0:T(8,128)(2,1)S(1)} %get-tuple-element.31.proj_all, f32[3,7,512]{2,1,0:T(8,128)S(1)} %bitcast.16, ...), custom_call_target="tpu_custom_call" | custom-call | flops 536870912 | bytes 5685248 | tf_op jit(solution)/shard_map/pallas_call | solution.py:233
  70.6 3.3 %collective-permute-done.9.refs_2_ = bf16[128,2048]{1,0:T(8,128)(2,1)S(1)} collective-permute-done((bf16[128,2048]{1,0:T(8,128)(2,1)}, bf16[128,2048]{1,0:T(8,128)(2,1)S(1)}, u32[]{:S(2)}, u32[]{:S(2)}) %collective-permute-start.9) | collective-permute-done | bytes 524320 | tf_op jit(solution)/shard_map/ppermute | solution.py:253
  73.9 2.1 %collective-permute-done.8.refs_1_ = bf16[128,2048]{1,0:T(8,128)(2,1)S(1)} collective-permute-done((bf16[128,2048]{1,0:T(8,128)(2,1)}, bf16[128,2048]{1,0:T(8,128)(2,1)S(1)}, u32[]{:S(2)}, u32[]{:S(2)}) %collective-permute-start.8) | collective-permute-done | bytes 524320 | tf_op jit(solution)/shard_map/ppermute | solution.py:253
  76.0 5.3 %shard_map.67 = (bf16[2,3,256,512]{3,2,1,0:T(8,128)(2,1)S(1)}, bf16[2,3,144,512]{3,2,1,0:T(8,128)(2,1)S(1)}) custom-call(bf16[128,2048]{1,0:T(8,128)(2,1)S(1)} %collective-permute-done.7.refs_0_, bf16[128,2048]{1,0:T(8,128)(2,1)S(1)} %collective-permute-done.8.refs_1_, bf16[128,2048]{1,0:T(8,128)(2,1)S(1)} %collective-permute-done.9.refs_2_, ...), custom_call_target="tpu_custom_call" | custom-call | flops 3221225472 | bytes 11010048 | tf_op jit(solution)/shard_map/pallas_call | solution.py:133
  82.6 2.1 %collective-permute-done.12.refs_0_ = bf16[128,2048]{1,0:T(8,128)(2,1)S(1)} collective-permute-done((bf16[128,2048]{1,0:T(8,128)(2,1)S(1)}, bf16[128,2048]{1,0:T(8,128)(2,1)S(1)}, u32[]{:S(2)}, u32[]{:S(2)}) %collective-permute-start.12) | collective-permute-done | bytes 524320 | tf_op jit(solution)/shard_map/ppermute | solution.py:253
  86.2 3.7 %shard_map.68 = (bf16[1,3,256,512]{3,2,1,0:T(8,128)(2,1)S(1)}, bf16[1,3,144,512]{3,2,1,0:T(8,128)(2,1)S(1)}) custom-call(bf16[128,2048]{1,0:T(8,128)(2,1)S(1)} %collective-permute-done.12.refs_0_, bf16[128,2048]{1,0:T(8,128)(2,1)S(1)} %collective-permute-done.13.refs_1_, bf16[2048,512]{1,0:T(8,128)(2,1)S(1)} %copy-done.2, ...), custom_call_target="tpu_custom_call" | custom-call | flops 1610612736 | bytes 8650752 | tf_op jit(solution)/shard_map/pallas_call | solution.py:133
  91.8 7.5 %shard_map.69 = (bf16[256,512]{1,0:T(8,128)(2,1)S(1)}, bf16[256,512]{1,0:T(8,128)(2,1)S(1)}) custom-call(s32[2,384,1]{2,1,0:T(8,128)S(1)} %pad_add_fusion.pos_all, bf16[2,3,144,512]{3,2,1,0:T(8,128)(2,1)S(1)} %collective-permute-done.11.halo_all, bf16[2,3,256,512]{3,2,1,0:T(8,128)(2,1)S(1)} %get-tuple-element.48.proj_all, f32[3,7,512]{2,1,0:T(8,128)S(1)} %bitcast.17, ...), custom_call_target="tpu_custom_call" | custom-call | flops 1073741824 | bytes 9273344 | tf_op jit(solution)/shard_map/pallas_call | solution.py:233
  99.3 3.6 %shard_map.70 = bf16[256,512]{1,0:T(8,128)(2,1)S(1)} custom-call(s32[1,384,1]{2,1,0:T(8,128)S(1)} %reshape_subtract_fusion.pos_all, bf16[1,3,144,512]{3,2,1,0:T(8,128)(2,1)S(1)} %collective-permute-done.17.halo_all, bf16[1,3,256,512]{3,2,1,0:T(8,128)(2,1)S(1)} %get-tuple-element.54.proj_all, f32[3,7,512]{2,1,0:T(8,128)S(1)} %bitcast.18, ...), custom_call_target="tpu_custom_call" | custom-call | flops 536870912 | bytes 5685248 | tf_op jit(solution)/shard_map/pallas_call | solution.py:233
  106.5 4.5 %collective-permute-done.18 = bf16[256,512]{1,0:T(8,128)(2,1)S(1)} collective-permute-done((bf16[256,512]{1,0:T(8,128)(2,1)S(1)}, bf16[256,512]{1,0:T(8,128)(2,1)S(1)}, u32[]{:S(2)}, u32[]{:S(2)}) %collective-permute-start.18) | collective-permute-done | bytes 262176 | tf_op jit(solution)/shard_map/ppermute | solution.py:253
  111.0 2.3 %fusion.2 = f32[256,2048]{1,0:T(8,128)S(1)} fusion(bf16[256,512]{1,0:T(8,128)(2,1)S(1)} %collective-permute-done.18, bf16[2048,2048]{1,0:T(8,128)(2,1)} %param.11, s32[]{:T(128)S(6)} %select_n.65), kind=kOutput, calls=%fused_computation.4 | convolution fusion | flops 536870912 | bytes 4456452 | tf_op jit(solution)/shard_map/dot_general | solution.py:330
  113.3 3.3 %collective-permute-done.14 = bf16[256,512]{1,0:T(8,128)(2,1)S(1)} collective-permute-done((bf16[256,512]{1,0:T(8,128)(2,1)S(1)}, bf16[256,512]{1,0:T(8,128)(2,1)S(1)}, u32[]{:S(2)}, u32[]{:S(2)}) %collective-permute-start.14) | collective-permute-done | bytes 262176 | tf_op jit(solution)/shard_map/ppermute | solution.py:253
  116.6 2.0 %collective-permute-done.15 = bf16[256,512]{1,0:T(8,128)(2,1)S(1)} collective-permute-done((bf16[256,512]{1,0:T(8,128)(2,1)S(1)}, bf16[256,512]{1,0:T(8,128)(2,1)S(1)}, u32[]{:S(2)}, u32[]{:S(2)}) %collective-permute-start.15) | collective-permute-done | bytes 262176 | tf_op jit(solution)/shard_map/ppermute | solution.py:253
  118.6 5.6 %fusion.1 = bf16[256,2048]{1,0:T(8,128)(2,1)} fusion(f32[256,2048]{1,0:T(8,128)S(1)} %fusion.2, bf16[1536,2048]{1,0:T(8,128)(2,1)} %pad_maximum_fusion, bf16[256,2048]{1,0:T(8,128)(2,1)S(1)} %copy-done.6, bf16[256,512]{1,0:T(8,128)(2,1)S(1)} %collective-permute-done.15, bf16[256,512]{1,0:T(8,128)(2,1)S(1)} %collective-permute-done.14, ...), kind=kOutput, calls=%fused_computation.3 | convolution fusion | flops 1615069184 | bytes 11272192 | tf_op jit(solution)/shard_map/dot_general | solution.py:327
  (67 shorter events, 28.6 us)
Async XLA Ops:
  0.0 14.8 %copy-start = (bf16[128,128]{1,0:T(8,128)(2,1)S(1)}, bf16[128,128]{1,0:T(8,128)(2,1)}, u32[]{:S(2)}) copy-start(bf16[128,128]{1,0:T(8,128)(2,1)} %param.10) | copy-start | bytes 98308
  0.0 44.7 %collective-permute-start.16 = (s32[1,4]{1,0:T(1,128)}, s32[1,4]{1,0:T(1,128)}, u32[]{:S(2)}, u32[]{:S(2)}) collective-permute-start(s32[1,4]{1,0:T(1,128)} %param.7), channel_id=1, source_target_pairs={{0,24},{8,16},{16,8},{24,0},{1,25},{9,17},{17,9},{25,1},{2,26},{10... | collective-permute-start | bytes 56 | tf_op jit(solution)/shard_map/ppermute | solution.py:253
  3.9 41.6 %collective-permute-start.6 = (s32[1,4]{1,0:T(1,128)}, s32[1,4]{1,0:T(1,128)}, u32[]{:S(2)}, u32[]{:S(2)}) collective-permute-start(s32[1,4]{1,0:T(1,128)} %param.7), channel_id=1, source_target_pairs={{0,16},{8,24},{16,0},{24,8},{1,17},{9,25},{17,1},{25,9},{2,18},{10... | collective-permute-start | bytes 56 | tf_op jit(solution)/shard_map/ppermute | solution.py:253
  4.4 41.9 %collective-permute-start.5 = (s32[1,4]{1,0:T(1,128)}, s32[1,4]{1,0:T(1,128)S(1)}, u32[]{:S(2)}, u32[]{:S(2)}) collective-permute-start(s32[1,4]{1,0:T(1,128)} %param.7), channel_id=1, source_target_pairs={{0,8},{8,0},{16,24},{24,16},{1,9},{9,1},{17,25},{25,17},{2,10},{10... | collective-permute-start | bytes 56 | tf_op jit(solution)/shard_map/ppermute | solution.py:253
  4.5 6.4 %copy-start.8 = (s32[1,4]{1,0:T(1,128)S(1)}, s32[1,4]{1,0:T(1,128)}, u32[]{:S(2)}) copy-start(s32[1,4]{1,0:T(1,128)} %param.7) | copy-start | bytes 52
  7.6 24.5 %collective-permute-start = (bf16[2048,256]{1,0:T(8,128)(2,1)}, bf16[2048,256]{1,0:T(8,128)(2,1)S(1)}, u32[]{:S(2)}, u32[]{:S(2)}) collective-permute-start(bf16[2048,256]{1,0:T(8,128)(2,1)} %get-tuple-element.63), channel_id=1, source_target_pairs={{0,8},{8,0},{16,24},{24,16},{1,9},{9,1},{17,25},{25,17},{2,10},{10... | collective-permute-start | bytes 3145736 | tf_op jit(solution)/shard_map/ppermute | solution.py:253
  9.5 24.1 %collective-permute-start.2 = (bf16[2048,256]{1,0:T(8,128)(2,1)}, bf16[2048,256]{1,0:T(8,128)(2,1)}, u32[]{:S(2)}, u32[]{:S(2)}) collective-permute-start(bf16[2048,256]{1,0:T(8,128)(2,1)} %get-tuple-element.62), channel_id=1, source_target_pairs={{0,16},{8,24},{16,0},{24,8},{1,17},{9,25},{17,1},{25,9},{2,18},{10... | collective-permute-start | bytes 3145736 | tf_op jit(solution)/shard_map/ppermute | solution.py:253
  16.6 4.1 %copy-start.5 = (bf16[256,2048]{1,0:T(8,128)(2,1)S(1)}, bf16[256,2048]{1,0:T(8,128)(2,1)}, u32[]{:S(2)}) copy-start(bf16[256,2048]{1,0:T(8,128)(2,1)} %param.6) | copy-start | bytes 3145732
  32.1 18.3 %collective-permute-start.1 = (bf16[2048,256]{1,0:T(8,128)(2,1)S(1)}, bf16[2048,256]{1,0:T(8,128)(2,1)}, u32[]{:S(2)}, u32[]{:S(2)}) collective-permute-start(bf16[2048,256]{1,0:T(8,128)(2,1)S(1)} %collective-permute-done.refs_3_.refs_5_), channel_id=1, source_target_pairs={{0,1},{1,0},{2,3},{3,2},{4,5},{5,4},{6,7},{7,6},{8,9},{9,8},{10,11... | collective-permute-start | bytes 3145736 | tf_op jit(solution)/shard_map/ppermute | solution.py:257
  33.5 18.2 %collective-permute-start.3 = (bf16[2048,256]{1,0:T(8,128)(2,1)}, bf16[2048,256]{1,0:T(8,128)(2,1)}, u32[]{:S(2)}, u32[]{:S(2)}) collective-permute-start(bf16[2048,256]{1,0:T(8,128)(2,1)} %collective-permute-done.2.refs_5_.refs_7_), channel_id=1, source_target_pairs={{0,1},{1,0},{2,3},{3,2},{4,5},{5,4},{6,7},{7,6},{8,9},{9,8},{10,11... | collective-permute-start | bytes 3145736 | tf_op jit(solution)/shard_map/ppermute | solution.py:257
  47.7 14.9 %collective-permute-start.10 = (bf16[128,2048]{1,0:T(8,128)(2,1)}, bf16[128,2048]{1,0:T(8,128)(2,1)S(1)}, u32[]{:S(2)}, u32[]{:S(2)}) collective-permute-start(bf16[128,2048]{1,0:T(8,128)(2,1)} %get-tuple-element.33.refs_1_), channel_id=1, source_target_pairs={{0,16},{8,24},{16,0},{24,8},{1,17},{9,25},{17,1},{25,9},{2,18},{10... | collective-permute-start | bytes 1572872 | tf_op jit(solution)/shard_map/ppermute | solution.py:253
  49.2 24.6 %collective-permute-start.9 = (bf16[128,2048]{1,0:T(8,128)(2,1)}, bf16[128,2048]{1,0:T(8,128)(2,1)S(1)}, u32[]{:S(2)}, u32[]{:S(2)}) collective-permute-start(bf16[128,2048]{1,0:T(8,128)(2,1)} %get-tuple-element.34.refs_0_), channel_id=1, source_target_pairs={{0,16},{8,24},{16,0},{24,8},{1,17},{9,25},{17,1},{25,9},{2,18},{10... | collective-permute-start | bytes 1572872 | tf_op jit(solution)/shard_map/ppermute | solution.py:253
  49.7 15.0 %collective-permute-start.7 = (bf16[128,2048]{1,0:T(8,128)(2,1)}, bf16[128,2048]{1,0:T(8,128)(2,1)S(1)}, u32[]{:S(2)}, u32[]{:S(2)}) collective-permute-start(bf16[128,2048]{1,0:T(8,128)(2,1)} %get-tuple-element.34.refs_0_), channel_id=1, source_target_pairs={{0,8},{8,0},{16,24},{24,16},{1,9},{9,1},{17,25},{25,17},{2,10},{10... | collective-permute-start | bytes 1572872 | tf_op jit(solution)/shard_map/ppermute | solution.py:253
  50.4 25.6 %collective-permute-start.8 = (bf16[128,2048]{1,0:T(8,128)(2,1)}, bf16[128,2048]{1,0:T(8,128)(2,1)S(1)}, u32[]{:S(2)}, u32[]{:S(2)}) collective-permute-start(bf16[128,2048]{1,0:T(8,128)(2,1)} %get-tuple-element.33.refs_1_), channel_id=1, source_target_pairs={{0,8},{8,0},{16,24},{24,16},{1,9},{9,1},{17,25},{25,17},{2,10},{10... | collective-permute-start | bytes 1572872 | tf_op jit(solution)/shard_map/ppermute | solution.py:253
  59.1 7.9 %collective-permute-start.4 = (bf16[1,3,144,512]{3,2,1,0:T(8,128)(2,1)S(1)}, bf16[1,3,144,512]{3,2,1,0:T(8,128)(2,1)S(1)}, u32[]{:S(2)}, u32[]{:S(2)}) collective-permute-start(bf16[1,3,144,512]{3,2,1,0:T(8,128)(2,1)S(1)} %get-tuple-element.30), channel_id=1, source_target_pairs={{0,1},{1,2},{2,3},{3,4},{4,5},{5,6},{6,7},{8,9},{9,10},{10,11},{11... | collective-permute-start | bytes 1327112 | tf_op jit(solution)/shard_map/ppermute | solution.py:14
  64.8 20.0 %collective-permute-start.12 = (bf16[128,2048]{1,0:T(8,128)(2,1)S(1)}, bf16[128,2048]{1,0:T(8,128)(2,1)S(1)}, u32[]{:S(2)}, u32[]{:S(2)}) collective-permute-start(bf16[128,2048]{1,0:T(8,128)(2,1)S(1)} %collective-permute-done.7.refs_0_), channel_id=1, source_target_pairs={{0,16},{8,24},{16,0},{24,8},{1,17},{9,25},{17,1},{25,9},{2,18},{10... | collective-permute-start | bytes 1572872 | tf_op jit(solution)/shard_map/ppermute | solution.py:253
  66.3 19.9 %collective-permute-start.13 = (bf16[128,2048]{1,0:T(8,128)(2,1)S(1)}, bf16[128,2048]{1,0:T(8,128)(2,1)S(1)}, u32[]{:S(2)}, u32[]{:S(2)}) collective-permute-start(bf16[128,2048]{1,0:T(8,128)(2,1)S(1)} %collective-permute-done.10.refs_3_), channel_id=1, source_target_pairs={{0,8},{8,0},{16,24},{24,16},{1,9},{9,1},{17,25},{25,17},{2,10},{10... | collective-permute-start | bytes 1572872 | tf_op jit(solution)/shard_map/ppermute | solution.py:253
  70.6 15.6 %copy-start.2 = (bf16[2048,512]{1,0:T(8,128)(2,1)S(1)}, bf16[2048,512]{1,0:T(8,128)(2,1)}, u32[]{:S(2)}) copy-start(bf16[2048,512]{1,0:T(8,128)(2,1)} %constant_dynamic-slice_fusion.7.refs_2_.refs_4_) | copy-start | bytes 6291460
  81.3 10.5 %collective-permute-start.11 = (bf16[2,3,144,512]{3,2,1,0:T(8,128)(2,1)S(1)}, bf16[2,3,144,512]{3,2,1,0:T(8,128)(2,1)S(1)}, u32[]{:S(2)}, u32[]{:S(2)}) collective-permute-start(bf16[2,3,144,512]{3,2,1,0:T(8,128)(2,1)S(1)} %get-tuple-element.41), channel_id=1, source_target_pairs={{0,1},{1,2},{2,3},{3,4},{4,5},{5,6},{6,7},{8,9},{9,10},{10,11},{11... | collective-permute-start | bytes 2654216 | tf_op jit(solution)/shard_map/ppermute | solution.py:14
  89.9 9.4 %collective-permute-start.17 = (bf16[1,3,144,512]{3,2,1,0:T(8,128)(2,1)S(1)}, bf16[1,3,144,512]{3,2,1,0:T(8,128)(2,1)S(1)}, u32[]{:S(2)}, u32[]{:S(2)}) collective-permute-start(bf16[1,3,144,512]{3,2,1,0:T(8,128)(2,1)S(1)} %get-tuple-element.46), channel_id=1, source_target_pairs={{0,1},{1,2},{2,3},{3,4},{4,5},{5,6},{6,7},{8,9},{9,10},{10,11},{11... | collective-permute-start | bytes 1327112 | tf_op jit(solution)/shard_map/ppermute | solution.py:14
  102.9 8.0 %collective-permute-start.18 = (bf16[256,512]{1,0:T(8,128)(2,1)S(1)}, bf16[256,512]{1,0:T(8,128)(2,1)S(1)}, u32[]{:S(2)}, u32[]{:S(2)}) collective-permute-start(bf16[256,512]{1,0:T(8,128)(2,1)S(1)} %shard_map.70), channel_id=1, source_target_pairs={{0,24},{8,16},{16,8},{24,0},{1,25},{9,17},{17,9},{25,1},{2,26},{10... | collective-permute-start | bytes 786440 | tf_op jit(solution)/shard_map/ppermute | solution.py:253
  104.5 12.1 %collective-permute-start.14 = (bf16[256,512]{1,0:T(8,128)(2,1)S(1)}, bf16[256,512]{1,0:T(8,128)(2,1)S(1)}, u32[]{:S(2)}, u32[]{:S(2)}) collective-permute-start(bf16[256,512]{1,0:T(8,128)(2,1)S(1)} %get-tuple-element.49), channel_id=1, source_target_pairs={{0,8},{8,0},{16,24},{24,16},{1,9},{9,1},{17,25},{25,17},{2,10},{10... | collective-permute-start | bytes 786440 | tf_op jit(solution)/shard_map/ppermute | solution.py:253
  106.0 12.6 %copy-start.6 = (bf16[256,2048]{1,0:T(8,128)(2,1)S(1)}, bf16[256,2048]{1,0:T(8,128)(2,1)}, u32[]{:S(2)}) copy-start(bf16[256,2048]{1,0:T(8,128)(2,1)} %param.6) | copy-start | bytes 3145732
  106.0 12.6 %collective-permute-start.15 = (bf16[256,512]{1,0:T(8,128)(2,1)S(1)}, bf16[256,512]{1,0:T(8,128)(2,1)S(1)}, u32[]{:S(2)}, u32[]{:S(2)}) collective-permute-start(bf16[256,512]{1,0:T(8,128)(2,1)S(1)} %get-tuple-element.50), channel_id=1, source_target_pairs={{0,16},{8,24},{16,0},{24,8},{1,17},{9,25},{17,1},{25,9},{2,18},{10... | collective-permute-start | bytes 786440 | tf_op jit(solution)/shard_map/ppermute | solution.py:253
  (4 other events, 4.6 us)

commit v3 on v2

--- a/solution.py
+++ b/solution.py
@@ -284,8 +284,7 @@
     x_high, y_low = swap(to_x[1], 1), swap(to_y[1], 2)
     blocks = (own, x_mine, x_other, y_mine, y_other)
 
-    lengths = [seq_lengths[0]] + [swap(seq_lengths, bit)[0] for bit in (1, 2, 3)]
-    row_ids = seq * rows - filter_len + jnp.arange(rows + filter_len, dtype=jnp.int32)
+    lengths = [seq_lengths] + [swap(seq_lengths, bit) for bit in (1, 2, 3)]
     taps = lax.dynamic_slice(
         short_filter.reshape(width, 3, 4, block), (0, 0, f, 0), (width, 3, 1, block)
     )[:, :, 0].transpose(1, 0, 2)
@@ -295,13 +294,6 @@
 
     halo_rows = filter_len + 16
 
-    def position_of(bit):
-        return positions(row_ids, jnp.cumsum(lengths[bit]) - lengths[bit])[:, None]
-
-    def mix_packs(bits, proj, halo):
-        pos = jnp.stack([position_of(bit) for bit in bits])
-        return mix(pos, halo, proj, taps, table, width, per_group)
-
     def rows_of(bit):
         return lax.dynamic_slice(out_weight, ((f ^ bit) * block, 0), (block, channels))
 
@@ -309,26 +301,41 @@
     halo_own = from_behind(tail, "seq", 1)
     to_d = lax.optimization_barrier((x_low, y_high, tail))
     d_low, d_high = swap(to_d[0], 2), swap(to_d[1], 1)
-    (own_out,) = mix_packs((0,), proj_own, halo_own)
-    first_weight = jnp.concatenate([rows_of(0), rows_of(1), rows_of(2)], axis=0)
-    others = lax.optimization_barrier((x_low, x_high, y_low, y_high, own_out, first_weight))
-    first_weight = others[5]
+
+    every = jnp.concatenate(lax.optimization_barrier((*lengths, tail))[:4], axis=0)
+    ids = jnp.arange(every.shape[1], dtype=jnp.int32)
+    earlier = (ids[:, None] < ids[None, :]).astype(jnp.int32)
+    starts = jnp.sum(every[:, :, None] * earlier[None], axis=1)
+    row_ids = seq * rows - filter_len + jnp.arange(rows + filter_len, dtype=jnp.int32)
+    before = jnp.where(starts[:, None, :] <= row_ids[None, :, None], starts[:, None, :], 0)
+    position = (row_ids[None, :] - jnp.max(before, axis=2))[:, :, None]
+
+    def mix_packs(first, last, proj, halo):
+        return mix(position[first:last], halo, proj, taps, table, width, per_group)
+
+    (own_out,) = mix_packs(0, 1, proj_own, halo_own)
+    weights = [rows_of(bit) for bit in range(4)]
+    total = tokens.astype(jnp.float32) + jnp.dot(
+        own_out, weights[0], preferred_element_type=jnp.float32
+    )
+    others = lax.optimization_barrier(
+        (x_low, x_high, y_low, y_high, own_out, total, *weights[1:])
+    )
+    total, weights[1:] = others[5], others[6:]
     proj_xy, tail_xy = project(others[:4], blocks, halo_rows)
     halo_xy = from_behind(tail_xy, "seq", 1)
     last = lax.optimization_barrier((d_low, d_high, tail_xy))
     proj_d, tail_d = project(last[:2], blocks, halo_rows)
     halo_d = from_behind(tail_d, "seq", 1)
-    x_out, y_out = mix_packs((1, 2), *lax.optimization_barrier((proj_xy, halo_xy, tail_d))[:2])
+    x_out, y_out = mix_packs(1, 3, *lax.optimization_barrier((proj_xy, halo_xy, tail_d))[:2])
     proj_d, halo_d, _ = lax.optimization_barrier((proj_d, halo_d, x_out))
-    (d_out,) = mix_packs((3,), proj_d, halo_d)
-    gated = [own_out, swap(x_out, 1), swap(y_out, 2), swap(d_out, 3)]
-
-    first = jnp.concatenate(gated[:3], axis=1)
-    result = tokens.astype(jnp.float32) + jnp.dot(
-        first, first_weight, preferred_element_type=jnp.float32
-    )
-    result = result + jnp.dot(gated[3], rows_of(3), preferred_element_type=jnp.float32)
-    return result.astype(jnp.bfloat16)
+    (d_out,) = mix_packs(3, 4, proj_d, halo_d)
+    x_back, y_back, d_back = swap(x_out, 1), swap(y_out, 2), swap(d_out, 3)
+    total = total + jnp.dot(x_back, weights[1], preferred_element_type=jnp.float32)
+    total = total + jnp.dot(y_back, weights[2], preferred_element_type=jnp.float32)
+    (total,) = lax.optimization_barrier((total,))
+    total = total + jnp.dot(d_back, weights[3], preferred_element_type=jnp.float32)
+    return total.astype(jnp.bfloat16)
 
 
 def solution(mesh):

time: 126 us -> 130 us (1.032)
  other arithmetic: 16.1 us -> 2.12 us
  waiting for transfers between devices: 34.3 us -> 42.6 us
  Pallas kernels: 28 us -> 32.9 us
  local copies, waits for them, and re-layouts: 15.4 us -> 19.4 us
  starting transfers between devices: 22.2 us -> 26 us
  matrix products: 7.87 us -> 5.97 us
    concatenate x1, other arithmetic: 11.2 us -> 0.68 us  [local_four(): jnp.concatenate(lax.optimization_barrier((*lengths, tail))[:4], axis=0)]
    ppermute x14, waiting for transfers between devices: 34.3 us -> 42.6 us  [swap(): return lax.ppermute(block, 'fsdp', [(i, i ^ bit) for i in range(4)])]
    ppermute x3, starting transfers between devices: 4.38 us -> 8.4 us  [from_behind(): return lax.ppermute(block, axis, route)]
    pallas_call x3, Pallas kernels: 14.7 us -> 18.1 us  [mix(): pl.pallas_call(functools.partial(mix_kernel, width, per_group), out_shape...]
    unnamed x20 -> x44, local copies, waits for them, and re-layouts: 3.77 us -> 6.8 us
    another operation x5 -> x0, other arithmetic: 2.52 us -> none
    le x4 -> x0, other arithmetic: 1.91 us -> none  [positions(): seq_starts[None, :] <= row_ids[:, None]]
    dot_general x2 -> x4, matrix products: 7.87 us -> 5.97 us  [the longest x1 3.82 us: local_four(): jnp.dot(own_out, weights[0], preferred_element_type=jnp.float32)]
  transfers between devices with their start and end apart: 19 -> 19, of which waited for: 11 -> 4; matrix products, arithmetic and copies ran while one was open for 24% -> 12% of each run, Pallas kernels for 20% -> 25%
where the time goes in v3:
time: 130 us; the launch traced here: 129 us
  waiting for transfers between devices  42.6 us (33%)
  Pallas kernels  32.9 us (25%)
  starting transfers between devices  26 us (20%)
  local copies, waits for them, and re-layouts  19.4 us (15%)
  matrix products  5.97 us (5%)
  other arithmetic  2.12 us (2%)
    ppermute x14, waiting for transfers between devices, swap(): return lax.ppermute(block, 'fsdp', [(i, i ^ bit) for i in range(4)])  42.6 us
    pallas_call x3, Pallas kernels, mix(): pl.pallas_call(functools.partial(mix_kernel, width, per_group), out_shape...  18.1 us
    ppermute x14, starting transfers between devices, swap(): return lax.ppermute(block, 'fsdp', [(i, i ^ bit) for i in range(4)])  17.6 us
    pallas_call x3, Pallas kernels, project(): pl.pallas_call(functools.partial(role_kernel, n), out_shape=[jax.ShapeDty...  14.1 us
    ppermute x3, starting transfers between devices, from_behind(): return lax.ppermute(block, axis, route)  8.4 us
    unnamed x44, local copies, waits for them, and re-layouts  6.8 us
    dynamic_slice x1, local copies, waits for them, and re-layouts, rows_of(): lax.dynamic_slice(out_weight, ((f ^ bit) * block, 0), (block, channels))  5.82 us
    dot_general x1, matrix products, local_four(): jnp.dot(own_out, weights[0], preferred_element_type=jnp.float32)  3.82 us
  transfers between devices with their start and end apart: 19, of which 4 were waited for; matrix products, arithmetic and copies ran while one was open for 12% of the time, Pallas kernels for 25%

profile of v3, /device:TPU:0, one launch (start us, length us, event | category | flops | bytes accessed | tf_op | source)
XLA Modules:
  0.0 129.2 jit_solution(7643978487580960147)
XLA Ops:
  0.0 3.0 %constant_dynamic-slice_fusion.6 = (bf16[2048,256]{1,0:T(8,128)(2,1)}, bf16[2048,256]{1,0:T(8,128)(2,1)}) fusion(bf16[2048,1536]{1,0:T(8,128)(2,1)} %param.8, s32[]{:T(128)S(6)} %select_n.45, s32[]{:T(128)S(6)} %select_n.43), kind=kLoop, calls=%fused_computation.16 | loop fusion | bytes 4194312 | tf_op jit(solution)/shard_map/dynamic_slice | solution.py:275
  3.0 3.0 %collective-permute-start.3 = (bf16[2048,256]{1,0:T(8,128)(2,1)}, bf16[2048,256]{1,0:T(8,128)(2,1)S(1)}, u32[]{:S(2)}, u32[]{:S(2)}) collective-permute-start(bf16[2048,256]{1,0:T(8,128)(2,1)} %get-tuple-element.72), channel_id=1, source_target_pairs={{0,16},{8,24},{16,0},{24,8},{1,17},{9,25},{17,1},{25,9},{2,18},{10... | collective-permute-start | bytes 3145736 | tf_op jit(solution)/shard_map/ppermute | solution.py:253
  6.0 1.5 %collective-permute-start = (bf16[2048,256]{1,0:T(8,128)(2,1)}, bf16[2048,256]{1,0:T(8,128)(2,1)}, u32[]{:S(2)}, u32[]{:S(2)}) collective-permute-start(bf16[2048,256]{1,0:T(8,128)(2,1)} %get-tuple-element.73), channel_id=1, source_target_pairs={{0,8},{8,0},{16,24},{24,16},{1,9},{9,1},{17,25},{25,17},{2,10},{10... | collective-permute-start | bytes 3145736 | tf_op jit(solution)/shard_map/ppermute | solution.py:253
  8.1 2.9 %collective-permute-start.8 = (s32[1,4]{1,0:T(1,128)S(1)}, s32[1,4]{1,0:T(1,128)}, u32[]{:S(2)}, u32[]{:S(2)}) collective-permute-start(s32[1,4]{1,0:T(1,128)S(1)} %copy-done.20), channel_id=1, source_target_pairs={{0,24},{8,16},{16,8},{24,0},{1,25},{9,17},{17,9},{25,1},{2,26},{10... | collective-permute-start | bytes 56 | tf_op jit(solution)/shard_map/ppermute | solution.py:253
  12.2 1.7 %constant_dynamic-slice_fusion.5.refs_2_.refs_4_ = bf16[2048,512]{1,0:T(8,128)(2,1)S(1)} fusion(bf16[2048,1536]{1,0:T(8,128)(2,1)} %param.8, s32[]{:T(128)S(6)} %select_n.46), kind=kLoop, calls=%fused_computation.15 | loop fusion | bytes 4194308 | tf_op jit(solution)/shard_map/dynamic_slice | solution.py:273
  13.9 15.5 %collective-permute-done.3.refs_5_.refs_7_ = bf16[2048,256]{1,0:T(8,128)(2,1)S(1)} collective-permute-done((bf16[2048,256]{1,0:T(8,128)(2,1)}, bf16[2048,256]{1,0:T(8,128)(2,1)S(1)}, u32[]{:S(2)}, u32[]{:S(2)}) %collective-permute-start.3) | collective-permute-done | bytes 1048608 | tf_op jit(solution)/shard_map/ppermute | solution.py:253
  29.4 1.6 %collective-permute-done.refs_3_.refs_5_ = bf16[2048,256]{1,0:T(8,128)(2,1)} collective-permute-done((bf16[2048,256]{1,0:T(8,128)(2,1)}, bf16[2048,256]{1,0:T(8,128)(2,1)}, u32[]{:S(2)}, u32[]{:S(2)}) %collective-permute-start) | collective-permute-done | bytes 1048608 | tf_op jit(solution)/shard_map/ppermute | solution.py:253
  31.0 5.8 %constant_dynamic-slice_fusion = (bf16[512,2048]{1,0:T(8,128)(2,1)}, bf16[512,2048]{1,0:T(8,128)(2,1)}, bf16[512,2048]{1,0:T(8,128)(2,1)}) fusion(bf16[2048,2048]{1,0:T(8,128)(2,1)} %param.11, s32[]{:T(128)S(6)} %select_n.53, s32[]{:T(128)S(6)} %select_n.51, s32[]{:T(128)S(6)} %select_n.52), kind=kLoop, calls=%fused_computation.9 | loop fusion | bytes 12582924 | tf_op jit(solution)/shard_map/dynamic_slice | solution.py:298
  39.9 4.1 %shard_map.64 = (bf16[1,3,256,512]{3,2,1,0:T(8,128)(2,1)S(1)}, bf16[1,3,144,512]{3,2,1,0:T(8,128)(2,1)}) custom-call(bf16[128,2048]{1,0:T(8,128)(2,1)} %get-tuple-element.39.refs_0_, bf16[128,2048]{1,0:T(8,128)(2,1)} %get-tuple-element.40.refs_1_, bf16[2048,512]{1,0:T(8,128)(2,1)S(1)} %constant_dynamic-slice_fusion.5.refs_2_.refs_4_, ...), custom_call_target="tpu_custom_call" | custom-call | flops 1610612736 | bytes 8650752 | tf_op jit(solution)/shard_map/pallas_call | solution.py:133
  45.0 1.5 %collective-permute-start.1 = (bf16[128,2048]{1,0:T(8,128)(2,1)}, bf16[128,2048]{1,0:T(8,128)(2,1)}, u32[]{:S(2)}, u32[]{:S(2)}) collective-permute-start(bf16[128,2048]{1,0:T(8,128)(2,1)} %get-tuple-element.39.refs_0_), channel_id=1, source_target_pairs={{0,8},{8,0},{16,24},{24,16},{1,9},{9,1},{17,25},{25,17},{2,10},{10... | collective-permute-start | bytes 1572872 | tf_op jit(solution)/shard_map/ppermute | solution.py:253
  47.0 2.1 %collective-permute-start.11 = (bf16[1,3,144,512]{3,2,1,0:T(8,128)(2,1)}, bf16[1,3,144,512]{3,2,1,0:T(8,128)(2,1)}, u32[]{:S(2)}, u32[]{:S(2)}) collective-permute-start(bf16[1,3,144,512]{3,2,1,0:T(8,128)(2,1)} %get-tuple-element.41), channel_id=1, source_target_pairs={{0,1},{1,2},{2,3},{3,4},{4,5},{5,6},{6,7},{8,9},{9,10},{10,11},{11... | collective-permute-start | bytes 1327112 | tf_op jit(solution)/shard_map/ppermute | solution.py:14
  50.1 13.6 %collective-permute-done.5.refs_3_ = bf16[128,2048]{1,0:T(8,128)(2,1)} collective-permute-done((bf16[128,2048]{1,0:T(8,128)(2,1)}, bf16[128,2048]{1,0:T(8,128)(2,1)}, u32[]{:S(2)}, u32[]{:S(2)}) %collective-permute-start.5) | collective-permute-done | bytes 524320 | tf_op jit(solution)/shard_map/ppermute | solution.py:253
  64.1 1.7 %collective-permute-start.14 = (bf16[128,2048]{1,0:T(8,128)(2,1)}, bf16[128,2048]{1,0:T(8,128)(2,1)S(1)}, u32[]{:S(2)}, u32[]{:S(2)}) collective-permute-start(bf16[128,2048]{1,0:T(8,128)(2,1)} %collective-permute-done.5.refs_3_), channel_id=1, source_target_pairs={{0,8},{8,0},{16,24},{24,16},{1,9},{9,1},{17,25},{25,17},{2,10},{10... | collective-permute-start | bytes 1572872 | tf_op jit(solution)/shard_map/ppermute | solution.py:253
  66.9 4.7 %shard_map.66 = bf16[256,512]{1,0:T(8,128)(2,1)S(1)} custom-call(s32[1,384,1]{2,1,0:T(8,128)S(1)} %copy.16.pos_all, bf16[1,3,144,512]{3,2,1,0:T(8,128)(2,1)} %collective-permute-done.11.halo_all, bf16[1,3,256,512]{3,2,1,0:T(8,128)(2,1)S(1)} %copy-done.10, f32[3,7,512]{2,1,0:T(8,128)S(1)} %bitcast.19, bf16[4096,256]{1,0:T(8,128)(2,1)S(1)} %shard_map.65.table_ref), custom_call_target="tpu_custom_call" | custom-call | flops 536870912 | bytes 5685248 | tf_op jit(solution)/shard_map/pallas_call | solution.py:233
  71.7 3.8 %convolution_add_fusion = f32[256,2048]{1,0:T(8,128)} fusion(bf16[256,512]{1,0:T(8,128)(2,1)S(1)} %shard_map.66, bf16[2048,2048]{1,0:T(8,128)(2,1)} %param.11, s32[]{:T(128)S(6)} %select_n.50, bf16[256,2048]{1,0:T(8,128)(2,1)S(1)} %copy-done.18), kind=kOutput, calls=%fused_computation | convolution fusion | flops 537919488 | bytes 5505028 | tf_op jit(solution)/shard_map/dot_general | solution.py:318
  75.5 6.2 %shard_map.67 = (bf16[2,3,256,512]{3,2,1,0:T(8,128)(2,1)S(1)}, bf16[2,3,144,512]{3,2,1,0:T(8,128)(2,1)}) custom-call(bf16[128,2048]{1,0:T(8,128)(2,1)} %collective-permute-done.1.refs_0_, bf16[128,2048]{1,0:T(8,128)(2,1)} %collective-permute-done.2.refs_1_, bf16[128,2048]{1,0:T(8,128)(2,1)} %collective-permute-done.4.refs_2_, ...), custom_call_target="tpu_custom_call" | custom-call | flops 3221225472 | bytes 11010048 | tf_op jit(solution)/shard_map/pallas_call | solution.py:133
  82.9 2.2 %collective-permute-start.12 = (bf16[2,3,144,512]{3,2,1,0:T(8,128)(2,1)}, bf16[2,3,144,512]{3,2,1,0:T(8,128)(2,1)}, u32[]{:S(2)}, u32[]{:S(2)}) collective-permute-start(bf16[2,3,144,512]{3,2,1,0:T(8,128)(2,1)} %get-tuple-element.53), channel_id=1, source_target_pairs={{0,1},{1,2},{2,3},{3,4},{4,5},{5,6},{6,7},{8,9},{9,10},{10,11},{11... | collective-permute-start | bytes 2654216 | tf_op jit(solution)/shard_map/ppermute | solution.py:14
  85.2 3.8 %shard_map.68 = (bf16[1,3,256,512]{3,2,1,0:T(8,128)(2,1)S(1)}, bf16[1,3,144,512]{3,2,1,0:T(8,128)(2,1)}) custom-call(bf16[128,2048]{1,0:T(8,128)(2,1)S(1)} %collective-permute-done.13.refs_0_, bf16[128,2048]{1,0:T(8,128)(2,1)S(1)} %collective-permute-done.14.refs_1_, bf16[2048,512]{1,0:T(8,128)(2,1)S(1)} %copy-done.2, ...), custom_call_target="tpu_custom_call" | custom-call | flops 1610612736 | bytes 8650752 | tf_op jit(solution)/shard_map/pallas_call | solution.py:133
  89.9 4.1 %collective-permute-start.17 = (bf16[1,3,144,512]{3,2,1,0:T(8,128)(2,1)}, bf16[1,3,144,512]{3,2,1,0:T(8,128)(2,1)}, u32[]{:S(2)}, u32[]{:S(2)}) collective-permute-start(bf16[1,3,144,512]{3,2,1,0:T(8,128)(2,1)} %get-tuple-element.58), channel_id=1, source_target_pairs={{0,1},{1,2},{2,3},{3,4},{4,5},{5,6},{6,7},{8,9},{9,10},{10,11},{11... | collective-permute-start | bytes 1327112 | tf_op jit(solution)/shard_map/ppermute | solution.py:14
  94.2 1.4 %copy-done.8 = bf16[2,3,256,512]{3,2,1,0:T(8,128)(2,1)S(1)} copy-done((bf16[2,3,256,512]{3,2,1,0:T(8,128)(2,1)S(1)}, bf16[2,3,256,512]{3,2,1,0:T(8,128)(2,1)}, u32[]{:S(2)}) %copy-start.8) | copy-done | bytes 1572888
  95.6 8.7 %shard_map.69 = (bf16[256,512]{1,0:T(8,128)(2,1)}, bf16[256,512]{1,0:T(8,128)(2,1)S(1)}) custom-call(s32[2,384,1]{2,1,0:T(8,128)S(1)} %copy.17.pos_all, bf16[2,3,144,512]{3,2,1,0:T(8,128)(2,1)} %collective-permute-done.12.halo_all, bf16[2,3,256,512]{3,2,1,0:T(8,128)(2,1)S(1)} %copy-done.8, f32[3,7,512]{2,1,0:T(8,128)S(1)} %bitcast.20, ...), custom_call_target="tpu_custom_call" | custom-call | flops 1073741824 | bytes 9273344 | tf_op jit(solution)/shard_map/pallas_call | solution.py:233
  106.1 4.7 %shard_map.70 = bf16[256,512]{1,0:T(8,128)(2,1)S(1)} custom-call(s32[1,384,1]{2,1,0:T(8,128)S(1)} %copy.18.pos_all, bf16[1,3,144,512]{3,2,1,0:T(8,128)(2,1)} %collective-permute-done.17.halo_all, bf16[1,3,256,512]{3,2,1,0:T(8,128)(2,1)S(1)} %copy-done.12, f32[3,7,512]{2,1,0:T(8,128)S(1)} %bitcast.21, bf16[4096,256]{1,0:T(8,128)(2,1)S(1)} %shard_map.65.table_ref), custom_call_target="tpu_custom_call" | custom-call | flops 536870912 | bytes 5685248 | tf_op jit(solution)/shard_map/pallas_call | solution.py:233
  110.9 2.5 %collective-permute-start.18 = (bf16[256,512]{1,0:T(8,128)(2,1)S(1)}, bf16[256,512]{1,0:T(8,128)(2,1)S(1)}, u32[]{:S(2)}, u32[]{:S(2)}) collective-permute-start(bf16[256,512]{1,0:T(8,128)(2,1)S(1)} %shard_map.70), channel_id=1, source_target_pairs={{0,24},{8,16},{16,8},{24,0},{1,25},{9,17},{17,9},{25,1},{2,26},{10... | collective-permute-start | bytes 786440 | tf_op jit(solution)/shard_map/ppermute | solution.py:253
  114.6 11.9 %collective-permute-done.16 = bf16[256,512]{1,0:T(8,128)(2,1)S(1)} collective-permute-done((bf16[256,512]{1,0:T(8,128)(2,1)S(1)}, bf16[256,512]{1,0:T(8,128)(2,1)S(1)}, u32[]{:S(2)}, u32[]{:S(2)}) %collective-permute-start.16) | collective-permute-done | bytes 262176 | tf_op jit(solution)/shard_map/ppermute | solution.py:253
  (90 shorter events, 16.8 us)
Async XLA Ops:
  0.0 11.0 %copy-start = (bf16[128,128]{1,0:T(8,128)(2,1)S(1)}, bf16[128,128]{1,0:T(8,128)(2,1)}, u32[]{:S(2)}) copy-start(bf16[128,128]{1,0:T(8,128)(2,1)} %param.10) | copy-start | bytes 98308
  3.0 26.3 %collective-permute-start.3 = (bf16[2048,256]{1,0:T(8,128)(2,1)}, bf16[2048,256]{1,0:T(8,128)(2,1)S(1)}, u32[]{:S(2)}, u32[]{:S(2)}) collective-permute-start(bf16[2048,256]{1,0:T(8,128)(2,1)} %get-tuple-element.72), channel_id=1, source_target_pairs={{0,16},{8,24},{16,0},{24,8},{1,17},{9,25},{17,1},{25,9},{2,18},{10... | collective-permute-start | bytes 3145736 | tf_op jit(solution)/shard_map/ppermute | solution.py:253
  6.0 24.9 %collective-permute-start = (bf16[2048,256]{1,0:T(8,128)(2,1)}, bf16[2048,256]{1,0:T(8,128)(2,1)}, u32[]{:S(2)}, u32[]{:S(2)}) collective-permute-start(bf16[2048,256]{1,0:T(8,128)(2,1)} %get-tuple-element.73), channel_id=1, source_target_pairs={{0,8},{8,0},{16,24},{24,16},{1,9},{9,1},{17,25},{25,17},{2,10},{10... | collective-permute-start | bytes 3145736 | tf_op jit(solution)/shard_map/ppermute | solution.py:253
  7.5 37.5 %collective-permute-start.6 = (s32[1,4]{1,0:T(1,128)S(1)}, s32[1,4]{1,0:T(1,128)S(1)}, u32[]{:S(2)}, u32[]{:S(2)}) collective-permute-start(s32[1,4]{1,0:T(1,128)S(1)} %copy-done.20), channel_id=1, source_target_pairs={{0,8},{8,0},{16,24},{24,16},{1,9},{9,1},{17,25},{25,17},{2,10},{10... | collective-permute-start | bytes 56 | tf_op jit(solution)/shard_map/ppermute | solution.py:253
  8.0 38.4 %collective-permute-start.7 = (s32[1,4]{1,0:T(1,128)S(1)}, s32[1,4]{1,0:T(1,128)}, u32[]{:S(2)}, u32[]{:S(2)}) collective-permute-start(s32[1,4]{1,0:T(1,128)S(1)} %copy-done.20), channel_id=1, source_target_pairs={{0,16},{8,24},{16,0},{24,8},{1,17},{9,25},{17,1},{25,9},{2,18},{10... | collective-permute-start | bytes 56 | tf_op jit(solution)/shard_map/ppermute | solution.py:253
  8.1 39.0 %collective-permute-start.8 = (s32[1,4]{1,0:T(1,128)S(1)}, s32[1,4]{1,0:T(1,128)}, u32[]{:S(2)}, u32[]{:S(2)}) collective-permute-start(s32[1,4]{1,0:T(1,128)S(1)} %copy-done.20), channel_id=1, source_target_pairs={{0,24},{8,16},{16,8},{24,0},{1,25},{9,17},{17,9},{25,1},{2,26},{10... | collective-permute-start | bytes 56 | tf_op jit(solution)/shard_map/ppermute | solution.py:253
  13.9 26.0 %copy-start.1 = (bf16[2048,512]{1,0:T(8,128)(2,1)}, bf16[2048,512]{1,0:T(8,128)(2,1)S(1)}, u32[]{:S(2)}) copy-start(bf16[2048,512]{1,0:T(8,128)(2,1)S(1)} %constant_dynamic-slice_fusion.5.refs_2_.refs_4_) | copy-start | bytes 6291460
  29.4 8.5 %collective-permute-start.10 = (bf16[2048,256]{1,0:T(8,128)(2,1)S(1)}, bf16[2048,256]{1,0:T(8,128)(2,1)S(1)}, u32[]{:S(2)}, u32[]{:S(2)}) collective-permute-start(bf16[2048,256]{1,0:T(8,128)(2,1)S(1)} %collective-permute-done.3.refs_5_.refs_7_), channel_id=1, source_target_pairs={{0,1},{1,0},{2,3},{3,2},{4,5},{5,4},{6,7},{7,6},{8,9},{9,8},{10,11... | collective-permute-start | bytes 3145736 | tf_op jit(solution)/shard_map/ppermute | solution.py:257
  31.0 7.6 %collective-permute-start.9 = (bf16[2048,256]{1,0:T(8,128)(2,1)}, bf16[2048,256]{1,0:T(8,128)(2,1)S(1)}, u32[]{:S(2)}, u32[]{:S(2)}) collective-permute-start(bf16[2048,256]{1,0:T(8,128)(2,1)} %collective-permute-done.refs_3_.refs_5_), channel_id=1, source_target_pairs={{0,1},{1,0},{2,3},{3,2},{4,5},{5,4},{6,7},{7,6},{8,9},{9,8},{10,11... | collective-permute-start | bytes 3145736 | tf_op jit(solution)/shard_map/ppermute | solution.py:257
  37.9 37.6 %collective-permute-start.4 = (bf16[128,2048]{1,0:T(8,128)(2,1)}, bf16[128,2048]{1,0:T(8,128)(2,1)}, u32[]{:S(2)}, u32[]{:S(2)}) collective-permute-start(bf16[128,2048]{1,0:T(8,128)(2,1)} %get-tuple-element.39.refs_0_), channel_id=1, source_target_pairs={{0,16},{8,24},{16,0},{24,8},{1,17},{9,25},{17,1},{25,9},{2,18},{10... | collective-permute-start | bytes 1572872 | tf_op jit(solution)/shard_map/ppermute | solution.py:253
  38.6 25.2 %collective-permute-start.5 = (bf16[128,2048]{1,0:T(8,128)(2,1)}, bf16[128,2048]{1,0:T(8,128)(2,1)}, u32[]{:S(2)}, u32[]{:S(2)}) collective-permute-start(bf16[128,2048]{1,0:T(8,128)(2,1)} %get-tuple-element.40.refs_1_), channel_id=1, source_target_pairs={{0,16},{8,24},{16,0},{24,8},{1,17},{9,25},{17,1},{25,9},{2,18},{10... | collective-permute-start | bytes 1572872 | tf_op jit(solution)/shard_map/ppermute | solution.py:253
  45.0 18.8 %collective-permute-start.1 = (bf16[128,2048]{1,0:T(8,128)(2,1)}, bf16[128,2048]{1,0:T(8,128)(2,1)}, u32[]{:S(2)}, u32[]{:S(2)}) collective-permute-start(bf16[128,2048]{1,0:T(8,128)(2,1)} %get-tuple-element.39.refs_0_), channel_id=1, source_target_pairs={{0,8},{8,0},{16,24},{24,16},{1,9},{9,1},{17,25},{25,17},{2,10},{10... | collective-permute-start | bytes 1572872 | tf_op jit(solution)/shard_map/ppermute | solution.py:253
  46.5 29.0 %collective-permute-start.2 = (bf16[128,2048]{1,0:T(8,128)(2,1)}, bf16[128,2048]{1,0:T(8,128)(2,1)}, u32[]{:S(2)}, u32[]{:S(2)}) collective-permute-start(bf16[128,2048]{1,0:T(8,128)(2,1)} %get-tuple-element.40.refs_1_), channel_id=1, source_target_pairs={{0,8},{8,0},{16,24},{24,16},{1,9},{9,1},{17,25},{25,17},{2,10},{10... | collective-permute-start | bytes 1572872 | tf_op jit(solution)/shard_map/ppermute | solution.py:253
  47.0 18.8 %collective-permute-start.11 = (bf16[1,3,144,512]{3,2,1,0:T(8,128)(2,1)}, bf16[1,3,144,512]{3,2,1,0:T(8,128)(2,1)}, u32[]{:S(2)}, u32[]{:S(2)}) collective-permute-start(bf16[1,3,144,512]{3,2,1,0:T(8,128)(2,1)} %get-tuple-element.41), channel_id=1, source_target_pairs={{0,1},{1,2},{2,3},{3,4},{4,5},{5,6},{6,7},{8,9},{9,10},{10,11},{11... | collective-permute-start | bytes 1327112 | tf_op jit(solution)/shard_map/ppermute | solution.py:14
  63.8 21.4 %collective-permute-start.13 = (bf16[128,2048]{1,0:T(8,128)(2,1)}, bf16[128,2048]{1,0:T(8,128)(2,1)S(1)}, u32[]{:S(2)}, u32[]{:S(2)}) collective-permute-start(bf16[128,2048]{1,0:T(8,128)(2,1)} %collective-permute-done.1.refs_0_), channel_id=1, source_target_pairs={{0,16},{8,24},{16,0},{24,8},{1,17},{9,25},{17,1},{25,9},{2,18},{10... | collective-permute-start | bytes 1572872 | tf_op jit(solution)/shard_map/ppermute | solution.py:253
  64.1 21.1 %collective-permute-start.14 = (bf16[128,2048]{1,0:T(8,128)(2,1)}, bf16[128,2048]{1,0:T(8,128)(2,1)S(1)}, u32[]{:S(2)}, u32[]{:S(2)}) collective-permute-start(bf16[128,2048]{1,0:T(8,128)(2,1)} %collective-permute-done.5.refs_3_), channel_id=1, source_target_pairs={{0,8},{8,0},{16,24},{24,16},{1,9},{9,1},{17,25},{25,17},{2,10},{10... | collective-permute-start | bytes 1572872 | tf_op jit(solution)/shard_map/ppermute | solution.py:253
  82.9 11.2 %collective-permute-start.12 = (bf16[2,3,144,512]{3,2,1,0:T(8,128)(2,1)}, bf16[2,3,144,512]{3,2,1,0:T(8,128)(2,1)}, u32[]{:S(2)}, u32[]{:S(2)}) collective-permute-start(bf16[2,3,144,512]{3,2,1,0:T(8,128)(2,1)} %get-tuple-element.53), channel_id=1, source_target_pairs={{0,1},{1,2},{2,3},{3,4},{4,5},{5,6},{6,7},{8,9},{9,10},{10,11},{11... | collective-permute-start | bytes 2654216 | tf_op jit(solution)/shard_map/ppermute | solution.py:14
  89.9 15.1 %collective-permute-start.17 = (bf16[1,3,144,512]{3,2,1,0:T(8,128)(2,1)}, bf16[1,3,144,512]{3,2,1,0:T(8,128)(2,1)}, u32[]{:S(2)}, u32[]{:S(2)}) collective-permute-start(bf16[1,3,144,512]{3,2,1,0:T(8,128)(2,1)} %get-tuple-element.58), channel_id=1, source_target_pairs={{0,1},{1,2},{2,3},{3,4},{4,5},{5,6},{6,7},{8,9},{9,10},{10,11},{11... | collective-permute-start | bytes 1327112 | tf_op jit(solution)/shard_map/ppermute | solution.py:14
  104.2 9.7 %collective-permute-start.15 = (bf16[256,512]{1,0:T(8,128)(2,1)}, bf16[256,512]{1,0:T(8,128)(2,1)S(1)}, u32[]{:S(2)}, u32[]{:S(2)}) collective-permute-start(bf16[256,512]{1,0:T(8,128)(2,1)} %get-tuple-element.61), channel_id=1, source_target_pairs={{0,8},{8,0},{16,24},{24,16},{1,9},{9,1},{17,25},{25,17},{2,10},{10... | collective-permute-start | bytes 786440 | tf_op jit(solution)/shard_map/ppermute | solution.py:253
  110.9 16.4 %collective-permute-start.18 = (bf16[256,512]{1,0:T(8,128)(2,1)S(1)}, bf16[256,512]{1,0:T(8,128)(2,1)S(1)}, u32[]{:S(2)}, u32[]{:S(2)}) collective-permute-start(bf16[256,512]{1,0:T(8,128)(2,1)S(1)} %shard_map.70), channel_id=1, source_target_pairs={{0,24},{8,16},{16,8},{24,0},{1,25},{9,17},{17,9},{25,1},{2,26},{10... | collective-permute-start | bytes 786440 | tf_op jit(solution)/shard_map/ppermute | solution.py:253
  113.4 13.2 %copy-start.15 = (bf16[512,2048]{1,0:T(8,128)(2,1)S(1)}, bf16[512,2048]{1,0:T(8,128)(2,1)}, u32[]{:S(2)}) copy-start(bf16[512,2048]{1,0:T(8,128)(2,1)} %get-tuple-element.64) | copy-start | bytes 6291460
  113.4 13.2 %copy-start.16 = (f32[256,2048]{1,0:T(8,128)S(1)}, f32[256,2048]{1,0:T(8,128)}, u32[]{:S(2)}) copy-start(f32[256,2048]{1,0:T(8,128)} %convolution_add_fusion) | copy-start | bytes 6291460
  113.4 13.2 %collective-permute-start.16 = (bf16[256,512]{1,0:T(8,128)(2,1)S(1)}, bf16[256,512]{1,0:T(8,128)(2,1)S(1)}, u32[]{:S(2)}, u32[]{:S(2)}) collective-permute-start(bf16[256,512]{1,0:T(8,128)(2,1)S(1)} %get-tuple-element.63), channel_id=1, source_target_pairs={{0,16},{8,24},{16,0},{24,8},{1,17},{9,25},{17,1},{25,9},{2,18},{10... | collective-permute-start | bytes 786440 | tf_op jit(solution)/shard_map/ppermute | solution.py:253
  114.6 12.7 %copy-start.13 = (bf16[512,2048]{1,0:T(8,128)(2,1)S(1)}, bf16[512,2048]{1,0:T(8,128)(2,1)}, u32[]{:S(2)}) copy-start(bf16[512,2048]{1,0:T(8,128)(2,1)} %get-tuple-element.68) | copy-start | bytes 6291460
  (16 other events, 64.6 us)

commit v4 on v3

--- a/solution.py
+++ b/solution.py
@@ -294,13 +294,12 @@
 
     halo_rows = filter_len + 16
 
-    def rows_of(bit):
-        return lax.dynamic_slice(out_weight, ((f ^ bit) * block, 0), (block, channels))
-
     proj_own, tail = project((low, high), blocks, halo_rows)
     halo_own = from_behind(tail, "seq", 1)
-    to_d = lax.optimization_barrier((x_low, y_high, tail))
-    d_low, d_high = swap(to_d[0], 2), swap(to_d[1], 1)
+    late_weight = lax.optimization_barrier((out_weight, tail))[0]
+
+    def rows_of(bit):
+        return lax.dynamic_slice(late_weight, ((f ^ bit) * block, 0), (block, channels))
 
     every = jnp.concatenate(lax.optimization_barrier((*lengths, tail))[:4], axis=0)
     ids = jnp.arange(every.shape[1], dtype=jnp.int32)
@@ -315,6 +314,8 @@
 
     (own_out,) = mix_packs(0, 1, proj_own, halo_own)
     weights = [rows_of(bit) for bit in range(4)]
+    to_d = lax.optimization_barrier((x_low, y_high, own_out, *weights[1:]))
+    d_low, d_high = swap(to_d[0], 2), swap(to_d[1], 1)
     total = tokens.astype(jnp.float32) + jnp.dot(
         own_out, weights[0], preferred_element_type=jnp.float32
     )
@@ -331,6 +332,7 @@
     proj_d, halo_d, _ = lax.optimization_barrier((proj_d, halo_d, x_out))
     (d_out,) = mix_packs(3, 4, proj_d, halo_d)
     x_back, y_back, d_back = swap(x_out, 1), swap(y_out, 2), swap(d_out, 3)
+    x_back, y_back = lax.optimization_barrier((x_back, y_back))
     total = total + jnp.dot(x_back, weights[1], preferred_element_type=jnp.float32)
     total = total + jnp.dot(y_back, weights[2], preferred_element_type=jnp.float32)
     (total,) = lax.optimization_barrier((total,))

time: 130 us -> 118 us (0.908)
  waiting for transfers between devices: 42.6 us -> 32.5 us
  other arithmetic: 2.12 us -> 0.22 us
  Pallas kernels: 32.9 us -> 34.7 us
  starting transfers between devices: 26 us -> 24.2 us
    ppermute x14, waiting for transfers between devices: 42.6 us -> 32.5 us  [swap(): return lax.ppermute(block, 'fsdp', [(i, i ^ bit) for i in range(4)])]
    ppermute x3, starting transfers between devices: 8.4 us -> 6.36 us  [from_behind(): return lax.ppermute(block, axis, route)]
    pallas_call x3, Pallas kernels: 14.1 us -> 16 us  [project(): pl.pallas_call(functools.partial(role_kernel, n), out_shape=[jax.ShapeDty...]
    dynamic_slice x1, local copies, waits for them, and re-layouts: 3.03 us -> 1.71 us  [local_four(): lax.dynamic_slice(in_weight, (0, (1 - odd) * 2 * block + core * half), (c...]
    unnamed x44 -> x34, local copies, waits for them, and re-layouts: 6.8 us -> 5.91 us
  transfers between devices with their start and end apart: 19 -> 19, of which waited for: 4 -> 7; matrix products, arithmetic and copies ran while one was open for 12% -> 14% of each run, Pallas kernels for 25% -> 30%
where the time goes in v4:
time: 118 us; the launch traced here: 117 us
  Pallas kernels  34.7 us (29%)
  waiting for transfers between devices  32.5 us (28%)
  starting transfers between devices  24.2 us (21%)
  local copies, waits for them, and re-layouts  18.3 us (16%)
  matrix products  6.96 us (6%)
    ppermute x14, waiting for transfers between devices, swap(): return lax.ppermute(block, 'fsdp', [(i, i ^ bit) for i in range(4)])  32.5 us
    pallas_call x3, Pallas kernels, mix(): pl.pallas_call(functools.partial(mix_kernel, width, per_group), out_shape...  18.1 us
    ppermute x14, starting transfers between devices, swap(): return lax.ppermute(block, 'fsdp', [(i, i ^ bit) for i in range(4)])  17.8 us
    pallas_call x3, Pallas kernels, project(): pl.pallas_call(functools.partial(role_kernel, n), out_shape=[jax.ShapeDty...  16 us
    ppermute x3, starting transfers between devices, from_behind(): return lax.ppermute(block, axis, route)  6.36 us
    unnamed x34, local copies, waits for them, and re-layouts  5.91 us
    dynamic_slice x1, local copies, waits for them, and re-layouts, rows_of(): lax.dynamic_slice(late_weight, ((f ^ bit) * block, 0), (block, channels))  5.88 us
    dot_general x1, matrix products, local_four(): jnp.dot(own_out, weights[0], preferred_element_type=jnp.float32)  3.78 us
  transfers between devices with their start and end apart: 19, of which 7 were waited for; matrix products, arithmetic and copies ran while one was open for 14% of the time, Pallas kernels for 30%

profile of v4, /device:TPU:0, one launch (start us, length us, event | category | flops | bytes accessed | tf_op | source)
XLA Modules:
  0.0 117.3 jit_solution(12905440539342658445)
XLA Ops:
  0.0 1.7 %constant_dynamic-slice_fusion.6 = (bf16[2048,256]{1,0:T(8,128)(2,1)S(1)}, bf16[2048,256]{1,0:T(8,128)(2,1)S(1)}) fusion(bf16[2048,1536]{1,0:T(8,128)(2,1)} %param.8, s32[]{:T(128)S(6)} %select_n.45, s32[]{:T(128)S(6)} %select_n.43), kind=kLoop, calls=%fused_computation.17 | loop fusion | bytes 4194312 | tf_op jit(solution)/shard_map/dynamic_slice | solution.py:275
  1.7 3.0 %collective-permute-start = (bf16[2048,256]{1,0:T(8,128)(2,1)S(1)}, bf16[2048,256]{1,0:T(8,128)(2,1)S(1)}, u32[]{:S(2)}, u32[]{:S(2)}) collective-permute-start(bf16[2048,256]{1,0:T(8,128)(2,1)S(1)} %get-tuple-element.79), channel_id=1, source_target_pairs={{0,8},{8,0},{16,24},{24,16},{1,9},{9,1},{17,25},{25,17},{2,10},{10... | collective-permute-start | bytes 3145736 | tf_op jit(solution)/shard_map/ppermute | solution.py:253
  4.7 1.5 %collective-permute-start.3 = (bf16[2048,256]{1,0:T(8,128)(2,1)S(1)}, bf16[2048,256]{1,0:T(8,128)(2,1)}, u32[]{:S(2)}, u32[]{:S(2)}) collective-permute-start(bf16[2048,256]{1,0:T(8,128)(2,1)S(1)} %get-tuple-element.78), channel_id=1, source_target_pairs={{0,16},{8,24},{16,0},{24,8},{1,17},{9,25},{17,1},{25,9},{2,18},{10... | collective-permute-start | bytes 3145736 | tf_op jit(solution)/shard_map/ppermute | solution.py:253
  6.8 2.9 %collective-permute-start.8 = (s32[1,4]{1,0:T(1,128)S(1)}, s32[1,4]{1,0:T(1,128)S(1)}, u32[]{:S(2)}, u32[]{:S(2)}) collective-permute-start(s32[1,4]{1,0:T(1,128)S(1)} %copy-done.15), channel_id=1, source_target_pairs={{0,24},{8,16},{16,8},{24,0},{1,25},{9,17},{17,9},{25,1},{2,26},{10... | collective-permute-start | bytes 56 | tf_op jit(solution)/shard_map/ppermute | solution.py:253
  10.9 17.0 %collective-permute-done.refs_3_.refs_5_ = bf16[2048,256]{1,0:T(8,128)(2,1)S(1)} collective-permute-done((bf16[2048,256]{1,0:T(8,128)(2,1)S(1)}, bf16[2048,256]{1,0:T(8,128)(2,1)S(1)}, u32[]{:S(2)}, u32[]{:S(2)}) %collective-permute-start) | collective-permute-done | bytes 1048608 | tf_op jit(solution)/shard_map/ppermute | solution.py:253
  27.9 1.6 %collective-permute-done.3.refs_5_.refs_7_ = bf16[2048,256]{1,0:T(8,128)(2,1)} collective-permute-done((bf16[2048,256]{1,0:T(8,128)(2,1)S(1)}, bf16[2048,256]{1,0:T(8,128)(2,1)}, u32[]{:S(2)}, u32[]{:S(2)}) %collective-permute-start.3) | collective-permute-done | bytes 1048608 | tf_op jit(solution)/shard_map/ppermute | solution.py:253
  30.5 1.8 %constant_dynamic-slice_fusion.5.refs_2_.refs_4_ = bf16[2048,512]{1,0:T(8,128)(2,1)S(1)} fusion(bf16[2048,1536]{1,0:T(8,128)(2,1)} %param.8, s32[]{:T(128)S(6)} %select_n.46), kind=kLoop, calls=%fused_computation.16 | loop fusion | bytes 4194308 | tf_op jit(solution)/shard_map/dynamic_slice | solution.py:273
  35.6 4.7 %shard_map.64 = (bf16[1,3,256,512]{3,2,1,0:T(8,128)(2,1)S(1)}, bf16[1,3,144,512]{3,2,1,0:T(8,128)(2,1)}) custom-call(bf16[128,2048]{1,0:T(8,128)(2,1)} %get-tuple-element.42.refs_0_, bf16[128,2048]{1,0:T(8,128)(2,1)} %get-tuple-element.43.refs_1_, bf16[2048,512]{1,0:T(8,128)(2,1)S(1)} %constant_dynamic-slice_fusion.5.refs_2_.refs_4_, ...), custom_call_target="tpu_custom_call" | custom-call | flops 1610612736 | bytes 8650752 | tf_op jit(solution)/shard_map/pallas_call | solution.py:133
  40.3 1.6 %collective-permute-start.4 = (bf16[128,2048]{1,0:T(8,128)(2,1)}, bf16[128,2048]{1,0:T(8,128)(2,1)}, u32[]{:S(2)}, u32[]{:S(2)}) collective-permute-start(bf16[128,2048]{1,0:T(8,128)(2,1)} %get-tuple-element.42.refs_0_), channel_id=1, source_target_pairs={{0,16},{8,24},{16,0},{24,8},{1,17},{9,25},{17,1},{25,9},{2,18},{10... | collective-permute-start | bytes 1572872 | tf_op jit(solution)/shard_map/ppermute | solution.py:253
  42.4 2.1 %collective-permute-start.11 = (bf16[1,3,144,512]{3,2,1,0:T(8,128)(2,1)}, bf16[1,3,144,512]{3,2,1,0:T(8,128)(2,1)}, u32[]{:S(2)}, u32[]{:S(2)}) collective-permute-start(bf16[1,3,144,512]{3,2,1,0:T(8,128)(2,1)} %get-tuple-element.44), channel_id=1, source_target_pairs={{0,1},{1,2},{2,3},{3,4},{4,5},{5,6},{6,7},{8,9},{9,10},{10,11},{11... | collective-permute-start | bytes 1327112 | tf_op jit(solution)/shard_map/ppermute | solution.py:14
  44.7 5.9 %constant_dynamic-slice_fusion = (bf16[512,2048]{1,0:T(8,128)(2,1)}, bf16[512,2048]{1,0:T(8,128)(2,1)}, bf16[512,2048]{1,0:T(8,128)(2,1)}) fusion(bf16[2048,2048]{1,0:T(8,128)(2,1)} %param.11, s32[]{:T(128)S(6)} %select_n.53, s32[]{:T(128)S(6)} %select_n.52, s32[]{:T(128)S(6)} %select_n.51), kind=kLoop, calls=%fused_computation.10 | loop fusion | bytes 12582924 | tf_op jit(solution)/shard_map/dynamic_slice | solution.py:302
  51.9 4.7 %shard_map.66 = bf16[256,512]{1,0:T(8,128)(2,1)S(1)} custom-call(s32[1,384,1]{2,1,0:T(8,128)S(1)} %copy.16.pos_all, bf16[1,3,144,512]{3,2,1,0:T(8,128)(2,1)} %collective-permute-done.11.halo_all, bf16[1,3,256,512]{3,2,1,0:T(8,128)(2,1)S(1)} %copy-done.6, f32[3,7,512]{2,1,0:T(8,128)S(1)} %bitcast.19, bf16[4096,256]{1,0:T(8,128)(2,1)S(1)} %shard_map.65.table_ref), custom_call_target="tpu_custom_call" | custom-call | flops 536870912 | bytes 5685248 | tf_op jit(solution)/shard_map/pallas_call | solution.py:233
  56.6 3.8 %convolution_add_fusion.1 = f32[256,2048]{1,0:T(8,128)} fusion(bf16[256,512]{1,0:T(8,128)(2,1)S(1)} %shard_map.66, bf16[2048,2048]{1,0:T(8,128)(2,1)} %param.11, s32[]{:T(128)S(6)} %select_n.50, bf16[256,2048]{1,0:T(8,128)(2,1)S(1)} %copy-done.14), kind=kOutput, calls=%fused_computation.1 | convolution fusion | flops 537919488 | bytes 5505028 | tf_op jit(solution)/shard_map/dot_general | solution.py:319
  60.4 5.3 %collective-permute-done.5.refs_3_ = bf16[128,2048]{1,0:T(8,128)(2,1)} collective-permute-done((bf16[128,2048]{1,0:T(8,128)(2,1)}, bf16[128,2048]{1,0:T(8,128)(2,1)}, u32[]{:S(2)}, u32[]{:S(2)}) %collective-permute-start.5) | collective-permute-done | bytes 524320 | tf_op jit(solution)/shard_map/ppermute | solution.py:253
  65.7 1.5 %collective-permute-start.13 = (bf16[128,2048]{1,0:T(8,128)(2,1)}, bf16[128,2048]{1,0:T(8,128)(2,1)S(1)}, u32[]{:S(2)}, u32[]{:S(2)}) collective-permute-start(bf16[128,2048]{1,0:T(8,128)(2,1)} %collective-permute-done.1.refs_0_), channel_id=1, source_target_pairs={{0,16},{8,24},{16,0},{24,8},{1,17},{9,25},{17,1},{25,9},{2,18},{10... | collective-permute-start | bytes 1572872 | tf_op jit(solution)/shard_map/ppermute | solution.py:253
  67.8 6.8 %shard_map.67 = (bf16[2,3,256,512]{3,2,1,0:T(8,128)(2,1)S(1)}, bf16[2,3,144,512]{3,2,1,0:T(8,128)(2,1)}) custom-call(bf16[128,2048]{1,0:T(8,128)(2,1)} %collective-permute-done.1.refs_0_, bf16[128,2048]{1,0:T(8,128)(2,1)} %collective-permute-done.2.refs_1_, bf16[128,2048]{1,0:T(8,128)(2,1)} %collective-permute-done.4.refs_2_, ...), custom_call_target="tpu_custom_call" | custom-call | flops 3221225472 | bytes 11010048 | tf_op jit(solution)/shard_map/pallas_call | solution.py:133
  75.8 2.2 %collective-permute-start.12 = (bf16[2,3,144,512]{3,2,1,0:T(8,128)(2,1)}, bf16[2,3,144,512]{3,2,1,0:T(8,128)(2,1)}, u32[]{:S(2)}, u32[]{:S(2)}) collective-permute-start(bf16[2,3,144,512]{3,2,1,0:T(8,128)(2,1)} %get-tuple-element.57), channel_id=1, source_target_pairs={{0,1},{1,2},{2,3},{3,4},{4,5},{5,6},{6,7},{8,9},{9,10},{10,11},{11... | collective-permute-start | bytes 2654216 | tf_op jit(solution)/shard_map/ppermute | solution.py:14
  80.1 4.4 %shard_map.68 = (bf16[1,3,256,512]{3,2,1,0:T(8,128)(2,1)S(1)}, bf16[1,3,144,512]{3,2,1,0:T(8,128)(2,1)}) custom-call(bf16[128,2048]{1,0:T(8,128)(2,1)S(1)} %collective-permute-done.13.refs_0_, bf16[128,2048]{1,0:T(8,128)(2,1)S(1)} %collective-permute-done.14.refs_1_, bf16[2048,512]{1,0:T(8,128)(2,1)S(1)} %copy-done.2, ...), custom_call_target="tpu_custom_call" | custom-call | flops 1610612736 | bytes 8650752 | tf_op jit(solution)/shard_map/pallas_call | solution.py:133
  85.4 2.1 %collective-permute-start.17 = (bf16[1,3,144,512]{3,2,1,0:T(8,128)(2,1)}, bf16[1,3,144,512]{3,2,1,0:T(8,128)(2,1)}, u32[]{:S(2)}, u32[]{:S(2)}) collective-permute-start(bf16[1,3,144,512]{3,2,1,0:T(8,128)(2,1)} %get-tuple-element.62), channel_id=1, source_target_pairs={{0,1},{1,2},{2,3},{3,4},{4,5},{5,6},{6,7},{8,9},{9,10},{10,11},{11... | collective-permute-start | bytes 1327112 | tf_op jit(solution)/shard_map/ppermute | solution.py:14
  89.1 8.7 %shard_map.69 = (bf16[256,512]{1,0:T(8,128)(2,1)}, bf16[256,512]{1,0:T(8,128)(2,1)S(1)}) custom-call(s32[2,384,1]{2,1,0:T(8,128)S(1)} %copy.17.pos_all, bf16[2,3,144,512]{3,2,1,0:T(8,128)(2,1)} %collective-permute-done.12.halo_all, bf16[2,3,256,512]{3,2,1,0:T(8,128)(2,1)S(1)} %copy-done.4, f32[3,7,512]{2,1,0:T(8,128)S(1)} %bitcast.20, ...), custom_call_target="tpu_custom_call" | custom-call | flops 1073741824 | bytes 9273344 | tf_op jit(solution)/shard_map/pallas_call | solution.py:233
  101.1 4.8 %shard_map.70 = bf16[256,512]{1,0:T(8,128)(2,1)S(1)} custom-call(s32[1,384,1]{2,1,0:T(8,128)S(1)} %copy.18.pos_all, bf16[1,3,144,512]{3,2,1,0:T(8,128)(2,1)} %collective-permute-done.17.halo_all, bf16[1,3,256,512]{3,2,1,0:T(8,128)(2,1)S(1)} %copy-done.8, f32[3,7,512]{2,1,0:T(8,128)S(1)} %bitcast.21, bf16[4096,256]{1,0:T(8,128)(2,1)S(1)} %shard_map.65.table_ref), custom_call_target="tpu_custom_call" | custom-call | flops 536870912 | bytes 5685248 | tf_op jit(solution)/shard_map/pallas_call | solution.py:233
  105.9 1.6 %collective-permute-start.18 = (bf16[256,512]{1,0:T(8,128)(2,1)S(1)}, bf16[256,512]{1,0:T(8,128)(2,1)S(1)}, u32[]{:S(2)}, u32[]{:S(2)}) collective-permute-start(bf16[256,512]{1,0:T(8,128)(2,1)S(1)} %shard_map.70), channel_id=1, source_target_pairs={{0,24},{8,16},{16,8},{24,0},{1,25},{9,17},{17,9},{25,1},{2,26},{10... | collective-permute-start | bytes 786440 | tf_op jit(solution)/shard_map/ppermute | solution.py:253
  109.3 6.3 %collective-permute-done.18 = bf16[256,512]{1,0:T(8,128)(2,1)S(1)} collective-permute-done((bf16[256,512]{1,0:T(8,128)(2,1)S(1)}, bf16[256,512]{1,0:T(8,128)(2,1)S(1)}, u32[]{:S(2)}, u32[]{:S(2)}) %collective-permute-start.18) | collective-permute-done | bytes 262176 | tf_op jit(solution)/shard_map/ppermute | solution.py:253
  115.6 1.7 %fusion = bf16[256,2048]{1,0:T(8,128)(2,1)} fusion(f32[256,2048]{1,0:T(8,128)S(1)} %add_add_fusion, bf16[256,512]{1,0:T(8,128)(2,1)S(1)} %collective-permute-done.18, bf16[512,2048]{1,0:T(8,128)(2,1)S(1)} %copy-done.9), kind=kOutput, calls=%fused_computation.2 | convolution fusion | flops 537919488 | bytes 5505024 | tf_op jit(solution)/shard_map/dot_general | solution.py:339
  (79 shorter events, 19.3 us)
Async XLA Ops:
  0.0 29.5 %copy-start = (bf16[128,128]{1,0:T(8,128)(2,1)S(1)}, bf16[128,128]{1,0:T(8,128)(2,1)}, u32[]{:S(2)}) copy-start(bf16[128,128]{1,0:T(8,128)(2,1)} %param.10) | copy-start | bytes 98308
  1.7 26.2 %collective-permute-start = (bf16[2048,256]{1,0:T(8,128)(2,1)S(1)}, bf16[2048,256]{1,0:T(8,128)(2,1)S(1)}, u32[]{:S(2)}, u32[]{:S(2)}) collective-permute-start(bf16[2048,256]{1,0:T(8,128)(2,1)S(1)} %get-tuple-element.79), channel_id=1, source_target_pairs={{0,8},{8,0},{16,24},{24,16},{1,9},{9,1},{17,25},{25,17},{2,10},{10... | collective-permute-start | bytes 3145736 | tf_op jit(solution)/shard_map/ppermute | solution.py:253
  4.7 24.7 %collective-permute-start.3 = (bf16[2048,256]{1,0:T(8,128)(2,1)S(1)}, bf16[2048,256]{1,0:T(8,128)(2,1)}, u32[]{:S(2)}, u32[]{:S(2)}) collective-permute-start(bf16[2048,256]{1,0:T(8,128)(2,1)S(1)} %get-tuple-element.78), channel_id=1, source_target_pairs={{0,16},{8,24},{16,0},{24,8},{1,17},{9,25},{17,1},{25,9},{2,18},{10... | collective-permute-start | bytes 3145736 | tf_op jit(solution)/shard_map/ppermute | solution.py:253
  6.2 34.1 %collective-permute-start.6 = (s32[1,4]{1,0:T(1,128)S(1)}, s32[1,4]{1,0:T(1,128)S(1)}, u32[]{:S(2)}, u32[]{:S(2)}) collective-permute-start(s32[1,4]{1,0:T(1,128)S(1)} %copy-done.15), channel_id=1, source_target_pairs={{0,8},{8,0},{16,24},{24,16},{1,9},{9,1},{17,25},{25,17},{2,10},{10... | collective-permute-start | bytes 56 | tf_op jit(solution)/shard_map/ppermute | solution.py:253
  6.8 35.1 %collective-permute-start.7 = (s32[1,4]{1,0:T(1,128)S(1)}, s32[1,4]{1,0:T(1,128)S(1)}, u32[]{:S(2)}, u32[]{:S(2)}) collective-permute-start(s32[1,4]{1,0:T(1,128)S(1)} %copy-done.15), channel_id=1, source_target_pairs={{0,16},{8,24},{16,0},{24,8},{1,17},{9,25},{17,1},{25,9},{2,18},{10... | collective-permute-start | bytes 56 | tf_op jit(solution)/shard_map/ppermute | solution.py:253
  6.8 35.6 %collective-permute-start.8 = (s32[1,4]{1,0:T(1,128)S(1)}, s32[1,4]{1,0:T(1,128)S(1)}, u32[]{:S(2)}, u32[]{:S(2)}) collective-permute-start(s32[1,4]{1,0:T(1,128)S(1)} %copy-done.15), channel_id=1, source_target_pairs={{0,24},{8,16},{16,8},{24,0},{1,25},{9,17},{17,9},{25,1},{2,26},{10... | collective-permute-start | bytes 56 | tf_op jit(solution)/shard_map/ppermute | solution.py:253
  27.9 5.7 %collective-permute-start.9 = (bf16[2048,256]{1,0:T(8,128)(2,1)S(1)}, bf16[2048,256]{1,0:T(8,128)(2,1)}, u32[]{:S(2)}, u32[]{:S(2)}) collective-permute-start(bf16[2048,256]{1,0:T(8,128)(2,1)S(1)} %collective-permute-done.refs_3_.refs_5_), channel_id=1, source_target_pairs={{0,1},{1,0},{2,3},{3,2},{4,5},{5,4},{6,7},{7,6},{8,9},{9,8},{10,11... | collective-permute-start | bytes 3145736 | tf_op jit(solution)/shard_map/ppermute | solution.py:257
  29.5 4.8 %collective-permute-start.10 = (bf16[2048,256]{1,0:T(8,128)(2,1)}, bf16[2048,256]{1,0:T(8,128)(2,1)}, u32[]{:S(2)}, u32[]{:S(2)}) collective-permute-start(bf16[2048,256]{1,0:T(8,128)(2,1)} %collective-permute-done.3.refs_5_.refs_7_), channel_id=1, source_target_pairs={{0,1},{1,0},{2,3},{3,2},{4,5},{5,4},{6,7},{7,6},{8,9},{9,8},{10,11... | collective-permute-start | bytes 3145736 | tf_op jit(solution)/shard_map/ppermute | solution.py:257
  32.4 8.0 %copy-start.1 = (bf16[2048,512]{1,0:T(8,128)(2,1)}, bf16[2048,512]{1,0:T(8,128)(2,1)S(1)}, u32[]{:S(2)}) copy-start(bf16[2048,512]{1,0:T(8,128)(2,1)S(1)} %constant_dynamic-slice_fusion.5.refs_2_.refs_4_) | copy-start | bytes 6291460
  33.6 26.9 %collective-permute-start.1 = (bf16[128,2048]{1,0:T(8,128)(2,1)}, bf16[128,2048]{1,0:T(8,128)(2,1)}, u32[]{:S(2)}, u32[]{:S(2)}) collective-permute-start(bf16[128,2048]{1,0:T(8,128)(2,1)} %get-tuple-element.42.refs_0_), channel_id=1, source_target_pairs={{0,8},{8,0},{16,24},{24,16},{1,9},{9,1},{17,25},{25,17},{2,10},{10... | collective-permute-start | bytes 1572872 | tf_op jit(solution)/shard_map/ppermute | solution.py:253
  34.2 26.2 %collective-permute-start.2 = (bf16[128,2048]{1,0:T(8,128)(2,1)}, bf16[128,2048]{1,0:T(8,128)(2,1)}, u32[]{:S(2)}, u32[]{:S(2)}) collective-permute-start(bf16[128,2048]{1,0:T(8,128)(2,1)} %get-tuple-element.43.refs_1_), channel_id=1, source_target_pairs={{0,8},{8,0},{16,24},{24,16},{1,9},{9,1},{17,25},{25,17},{2,10},{10... | collective-permute-start | bytes 1572872 | tf_op jit(solution)/shard_map/ppermute | solution.py:253
  40.3 10.3 %copy-start.5 = (bf16[1,3,256,512]{3,2,1,0:T(8,128)(2,1)}, bf16[1,3,256,512]{3,2,1,0:T(8,128)(2,1)S(1)}, u32[]{:S(2)}) copy-start(bf16[1,3,256,512]{3,2,1,0:T(8,128)(2,1)S(1)} %get-tuple-element.49.proj_all) | copy-start | bytes 2359300
  40.3 20.1 %collective-permute-start.4 = (bf16[128,2048]{1,0:T(8,128)(2,1)}, bf16[128,2048]{1,0:T(8,128)(2,1)}, u32[]{:S(2)}, u32[]{:S(2)}) collective-permute-start(bf16[128,2048]{1,0:T(8,128)(2,1)} %get-tuple-element.42.refs_0_), channel_id=1, source_target_pairs={{0,16},{8,24},{16,0},{24,8},{1,17},{9,25},{17,1},{25,9},{2,18},{10... | collective-permute-start | bytes 1572872 | tf_op jit(solution)/shard_map/ppermute | solution.py:253
  41.9 23.8 %collective-permute-start.5 = (bf16[128,2048]{1,0:T(8,128)(2,1)}, bf16[128,2048]{1,0:T(8,128)(2,1)}, u32[]{:S(2)}, u32[]{:S(2)}) collective-permute-start(bf16[128,2048]{1,0:T(8,128)(2,1)} %get-tuple-element.43.refs_1_), channel_id=1, source_target_pairs={{0,16},{8,24},{16,0},{24,8},{1,17},{9,25},{17,1},{25,9},{2,18},{10... | collective-permute-start | bytes 1572872 | tf_op jit(solution)/shard_map/ppermute | solution.py:253
  42.4 8.3 %collective-permute-start.11 = (bf16[1,3,144,512]{3,2,1,0:T(8,128)(2,1)}, bf16[1,3,144,512]{3,2,1,0:T(8,128)(2,1)}, u32[]{:S(2)}, u32[]{:S(2)}) collective-permute-start(bf16[1,3,144,512]{3,2,1,0:T(8,128)(2,1)} %get-tuple-element.44), channel_id=1, source_target_pairs={{0,1},{1,2},{2,3},{3,4},{4,5},{5,6},{6,7},{8,9},{9,10},{10,11},{11... | collective-permute-start | bytes 1327112 | tf_op jit(solution)/shard_map/ppermute | solution.py:14
  56.6 11.2 %copy-start.2 = (bf16[2048,512]{1,0:T(8,128)(2,1)S(1)}, bf16[2048,512]{1,0:T(8,128)(2,1)}, u32[]{:S(2)}) copy-start(bf16[2048,512]{1,0:T(8,128)(2,1)} %copy-done.1) | copy-start | bytes 6291460
  65.7 13.1 %collective-permute-start.13 = (bf16[128,2048]{1,0:T(8,128)(2,1)}, bf16[128,2048]{1,0:T(8,128)(2,1)S(1)}, u32[]{:S(2)}, u32[]{:S(2)}) collective-permute-start(bf16[128,2048]{1,0:T(8,128)(2,1)} %collective-permute-done.1.refs_0_), channel_id=1, source_target_pairs={{0,16},{8,24},{16,0},{24,8},{1,17},{9,25},{17,1},{25,9},{2,18},{10... | collective-permute-start | bytes 1572872 | tf_op jit(solution)/shard_map/ppermute | solution.py:253
  67.2 12.8 %collective-permute-start.14 = (bf16[128,2048]{1,0:T(8,128)(2,1)}, bf16[128,2048]{1,0:T(8,128)(2,1)S(1)}, u32[]{:S(2)}, u32[]{:S(2)}) collective-permute-start(bf16[128,2048]{1,0:T(8,128)(2,1)} %collective-permute-done.5.refs_3_), channel_id=1, source_target_pairs={{0,8},{8,0},{16,24},{24,16},{1,9},{9,1},{17,25},{25,17},{2,10},{10... | collective-permute-start | bytes 1572872 | tf_op jit(solution)/shard_map/ppermute | solution.py:253
  75.8 11.9 %collective-permute-start.12 = (bf16[2,3,144,512]{3,2,1,0:T(8,128)(2,1)}, bf16[2,3,144,512]{3,2,1,0:T(8,128)(2,1)}, u32[]{:S(2)}, u32[]{:S(2)}) collective-permute-start(bf16[2,3,144,512]{3,2,1,0:T(8,128)(2,1)} %get-tuple-element.57), channel_id=1, source_target_pairs={{0,1},{1,2},{2,3},{3,4},{4,5},{5,6},{6,7},{8,9},{9,10},{10,11},{11... | collective-permute-start | bytes 2654216 | tf_op jit(solution)/shard_map/ppermute | solution.py:14
  85.4 14.5 %collective-permute-start.17 = (bf16[1,3,144,512]{3,2,1,0:T(8,128)(2,1)}, bf16[1,3,144,512]{3,2,1,0:T(8,128)(2,1)}, u32[]{:S(2)}, u32[]{:S(2)}) collective-permute-start(bf16[1,3,144,512]{3,2,1,0:T(8,128)(2,1)} %get-tuple-element.62), channel_id=1, source_target_pairs={{0,1},{1,2},{2,3},{3,4},{4,5},{5,6},{6,7},{8,9},{9,10},{10,11},{11... | collective-permute-start | bytes 1327112 | tf_op jit(solution)/shard_map/ppermute | solution.py:14
  97.8 9.7 %collective-permute-start.15 = (bf16[256,512]{1,0:T(8,128)(2,1)}, bf16[256,512]{1,0:T(8,128)(2,1)S(1)}, u32[]{:S(2)}, u32[]{:S(2)}) collective-permute-start(bf16[256,512]{1,0:T(8,128)(2,1)} %get-tuple-element.65), channel_id=1, source_target_pairs={{0,8},{8,0},{16,24},{24,16},{1,9},{9,1},{17,25},{25,17},{2,10},{10... | collective-permute-start | bytes 786440 | tf_op jit(solution)/shard_map/ppermute | solution.py:253
  99.3 8.4 %collective-permute-start.16 = (bf16[256,512]{1,0:T(8,128)(2,1)S(1)}, bf16[256,512]{1,0:T(8,128)(2,1)S(1)}, u32[]{:S(2)}, u32[]{:S(2)}) collective-permute-start(bf16[256,512]{1,0:T(8,128)(2,1)S(1)} %get-tuple-element.66), channel_id=1, source_target_pairs={{0,16},{8,24},{16,0},{24,8},{1,17},{9,25},{17,1},{25,9},{2,18},{10... | collective-permute-start | bytes 786440 | tf_op jit(solution)/shard_map/ppermute | solution.py:253
  105.9 9.7 %collective-permute-start.18 = (bf16[256,512]{1,0:T(8,128)(2,1)S(1)}, bf16[256,512]{1,0:T(8,128)(2,1)S(1)}, u32[]{:S(2)}, u32[]{:S(2)}) collective-permute-start(bf16[256,512]{1,0:T(8,128)(2,1)S(1)} %shard_map.70), channel_id=1, source_target_pairs={{0,24},{8,16},{16,8},{24,0},{1,25},{9,17},{17,9},{25,1},{2,26},{10... | collective-permute-start | bytes 786440 | tf_op jit(solution)/shard_map/ppermute | solution.py:253
  108.5 7.1 %copy-start.9 = (bf16[512,2048]{1,0:T(8,128)(2,1)S(1)}, bf16[512,2048]{1,0:T(8,128)(2,1)}, u32[]{:S(2)}) copy-start(bf16[512,2048]{1,0:T(8,128)(2,1)} %get-tuple-element.74) | copy-start | bytes 6291460
  (11 other events, 30.4 us)
